TPU v7x, 128 devices: a whole 4x4x4 slice. The times are simulated.
128 devices in a mesh: lon: 16 (over x, z_lo, core), lat: 8 (over y, z_hi).
Axes of the slice: x: 4, y: 4, z: 4 (z_hi: 2, z_lo: 2; z = z_hi * 2 + z_lo), core: 2. Of those that a mesh axis runs over, the one named last changes fastest.
Arguments:
- tracers: bfloat16 [2, 4, 1024, 16384], P(None, None, 'lat', 'lon'), may hold values from -6 to 6
- interp: bfloat16 [1024, 256, 128], P('lat'), may hold values from -0.375 to 0.375
- lat_weight: float32 [1024, 128], P('lat', 'lon'), may hold values from 0 to 1
- lat_row: int32 [1024, 128], P('lat', 'lon'), may hold values from 0 to 1022, as said below
- lon_offset: int32 [1024, 128], P('lat', 'lon'), may hold values from -25 to 64, as said below
Outputs:
- advected: bfloat16 [2, 4, 1024, 16384], P(None, None, 'lat', 'lon')
Inputs may be any that keep to these rules, and one draw needn't show every extreme that they name: lat_row[j, b] is j - 1 or j, clipped to 0 .. 1022. For rows j < 1024 // 32 (departures across the pole) lon_offset[j, b] lies in 56 .. 64; for other rows, with q = 1 + [j < 128] + 2 * [j < 64], it lies in -(q - 1) * 8 - 1 .. (q - 1) * 8; both ends are taken in every row; over all rows the offsets reach max(64, 24).
All inputs are finite; a program needn't handle non-finite values.
Results may differ from a plain program's by a relative error of at most 0.001.
Values may be sent and summed in bfloat16 or wider, within the bound.
A program may use at most 128 MiB of HBM per device.

v0:
```python
import jax
import jax.numpy as jnp
from jax import lax
from jax.sharding import PartitionSpec as P

BLK = 128


def with_halo(value, sides, width):
    for axis, dim in sides:
        devices, length = (lax.axis_size(axis), value.shape[dim])
        up = [(i, (i + 1) % devices) for i in range(devices - 1)]
        down = [(j, i) for i, j in up]
        last = lax.slice_in_dim(value, length - width, length, axis=dim)
        initial = lax.slice_in_dim(value, 0, width, axis=dim)
        before = lax.ppermute(last, axis, up)
        after = lax.ppermute(initial, axis, down)
        value = jnp.concatenate([before, value, after], axis=dim)
    return value


def on_device(tracers, interp, lat_weight, lat_row, lon_offset):
    channels = tracers.shape[0] * tracers.shape[1]
    band_rows = tracers.shape[2]
    span_cols = tracers.shape[3]
    packed = tracers.reshape(channels, band_rows, span_cols)
    rimmed = with_halo(packed, (("lat", 1),), 1)
    shard_blocks = span_cols // BLK
    first_row = lax.axis_index("lat") * band_rows
    first_block = lax.axis_index("lon") * shard_blocks
    local_rows = lat_row - first_row + 1
    relative = lon_offset + jnp.arange(shard_blocks, dtype=jnp.int32)[None, :]
    window = lax.all_gather(rimmed, "lon", axis=2, tiled=True)
    total_blocks = window.shape[2] // BLK
    leading = jnp.mod(first_block + relative, total_blocks)
    trailing = jnp.mod(leading + 1, total_blocks)
    tiles = window.reshape(channels, band_rows + 2, window.shape[2] // BLK, BLK)
    lower = jnp.concatenate(
        [tiles[:, local_rows, leading], tiles[:, local_rows, trailing]], axis=-1
    )
    upper_rows = local_rows + 1
    upper = jnp.concatenate(
        [tiles[:, upper_rows, leading], tiles[:, upper_rows, trailing]], axis=-1
    )
    south_part = jnp.einsum("crbk,rkn->crbn", lower, interp, preferred_element_type=jnp.float32)
    north_part = jnp.einsum("crbk,rkn->crbn", upper, interp, preferred_element_type=jnp.float32)
    blend = lat_weight[None, :, :, None]
    result = (1.0 - blend) * south_part + blend * north_part
    return result.reshape(tracers.shape).astype(jnp.bfloat16)


def solution(mesh):
    return jax.shard_map(
        on_device,
        mesh=mesh,
        in_specs=(
            P(None, None, "lat", "lon"),
            P("lat", None, None),
            P("lat", "lon"),
            P("lat", "lon"),
            P("lat", "lon"),
        ),
        out_specs=P(None, None, "lat", "lon"),
        check_vma=False,
    )
```

profile of v0, /device:TPU:1, one launch (start us, length us, event | category | flops | bytes accessed | tf_op | source)
XLA Modules:
  0.0 283.8 jit_solution(14043399701984592235)
XLA Ops:
  6.5 0.0 all-gather.2.cloned.1.call-start
  6.5 2.7 copy.10
  9.3 6.3 %collective-permute-start = (bf16[8,1,1024]{2,0,1:T(8,128)(2,1)S(1)}, bf16[8,1,1024]{2,0,1:T(8,128)(2,1)S(1)}, u32[]{:S(2)}, u32[]{:S(2)}) collective-permute-start(bf16[8,1,1024]{2,0,1:T(8,128)(2,1)S(1)} %get-tuple-element.5), channel_id=1, source_target_pairs={{0,1},{1,2},{2,3},{3,4},{4,5},{5,6},{6,7},{8,9},{9,10},{10,11},{11... | collective-permute-start | bytes 49160 | tf_op jit(solution)/shard_map/ppermute | solution.py:16
  15.6 1.3 collective-permute-start.1
  16.9 0.0 collective-permute-done
  16.9 4.7 %collective-permute-done.1 = bf16[8,1,1024]{2,0,1:T(8,128)(2,1)S(1)} collective-permute-done((bf16[8,1,1024]{2,0,1:T(8,128)(2,1)S(1)}, bf16[8,1,1024]{2,0,1:T(8,128)(2,1)S(1)}, u32[]{:S(2)}, u32[]{:S(2)}) %collective-permute-start.1) | collective-permute-done | bytes 16416 | tf_op jit(solution)/shard_map/ppermute | solution.py:17
  21.6 1.6 pad_maximum_fusion
  23.2 0.0 copy-start.2
  23.2 0.0 copy-start.3
  23.2 0.0 copy-start.1
  23.2 0.0 all-gather.2.cloned.1.call-update
  23.3 0.7 copy-done.2
  23.9 0.0 copy-done.3
  24.0 0.1 copy.20
  24.1 0.1 reshape.25
  24.2 0.1 copy.23
  24.3 0.1 reshape.31
  24.3 0.1 copy.13
  24.4 0.1 reshape.13
  24.5 0.1 copy.16
  24.6 0.1 reshape.19
  24.7 0.0 copy-done.1
  24.7 0.1 copy.19
  24.9 0.1 copy.9
  25.0 174.1 %all-gather.2.cloned.1.call-done = bf16[8,130,16384]{2,0,1:T(8,128)(2,1)} async-done(((bf16[8,130,1024]{2,0,1:T(8,128)(2,1)}), bf16[8,130,16384]{2,0,1:T(8,128)(2,1)}) %all-gather.2.cloned.1.call-update) | async-done | bytes 34078736 | tf_op jit(solution)/shard_map/all_gather | solution.py:33
  199.1 16.2 %gather_fusion.2 = bf16[1024,8,128]{2,1,0:T(8,128)(2,1)} fusion(bf16[8,130,128,128]{3,0,2,1:T(8,128)(2,1)} %bitcast.39, s32[1024]{0:T(1024)S(1)} %reshape.25), kind=kCustom, calls=%fused_computation.2 | custom fusion | bytes 4202496 | tf_op jit(solution)/shard_map/gather | solution.py:43
  215.3 16.1 %gather_fusion.3 = bf16[1024,8,128]{2,1,0:T(8,128)(2,1)} fusion(bf16[8,130,128,128]{3,0,2,1:T(8,128)(2,1)} %bitcast.40, s32[1024]{0:T(1024)S(1)} %reshape.31), kind=kCustom, calls=%fused_computation.3 | custom fusion | bytes 4202496 | tf_op jit(solution)/shard_map/gather | solution.py:43
  231.4 11.1 %gather_fusion = bf16[1024,8,128]{2,1,0:T(8,128)(2,1)S(1)} fusion(bf16[8,130,128,128]{3,0,2,1:T(8,128)(2,1)} %bitcast.41, s32[1024]{0:T(1024)S(1)} %reshape.13), kind=kCustom, calls=%fused_computation | custom fusion | bytes 4202496 | tf_op jit(solution)/shard_map/gather | solution.py:39
  242.5 16.2 %gather_fusion.1 = bf16[1024,8,128]{2,1,0:T(8,128)(2,1)} fusion(bf16[8,130,128,128]{3,0,2,1:T(8,128)(2,1)} %bitcast.42, s32[1024]{0:T(1024)S(1)} %reshape.19), kind=kCustom, calls=%fused_computation.1 | custom fusion | bytes 4202496 | tf_op jit(solution)/shard_map/gather | solution.py:39
  258.6 0.0 copy-start
  258.6 0.0 slice-start
  258.6 3.5 %copy_bitcast_fusion = (bf16[8,128,8,128]{3,2,0,1:T(8,128)(2,1)S(1)}, bf16[8,128,8,128]{3,2,0,1:T(8,128)(2,1)S(1)}) fusion(bf16[128,8,8,128]{3,2,1,0:T(8,128)(2,1)} %bitcast.37, bf16[128,8,8,128]{3,2,1,0:T(8,128)(2,1)} %bitcast.35), kind=kLoop, calls=%fused_computation.17 | loop fusion | bytes 8388608 | tf_op jit(solution)/shard_map/gather | solution.py:43
  262.2 0.0 copy-done
  262.2 0.0 slice-start.1
  262.2 3.3 %copy_bitcast_fusion.2 = (bf16[8,128,8,128]{3,2,0,1:T(8,128)(2,1)}, bf16[8,128,8,128]{3,2,0,1:T(8,128)(2,1)}) fusion(bf16[128,8,8,128]{3,2,1,0:T(8,128)(2,1)S(1)} %bitcast.36, bf16[128,8,8,128]{3,2,1,0:T(8,128)(2,1)S(1)} %bitcast.34), kind=kLoop, calls=%fused_computation.19 | loop fusion | bytes 8388608 | tf_op jit(solution)/shard_map/gather | solution.py:39
  265.5 0.0 slice-done
  265.5 0.0 slice-done.1
  265.5 1.4 fusion
  266.9 3.9 %fusion.10 = bf16[8,128,8,128]{3,2,0,1:T(8,128)(2,1)S(1)} fusion(f32[128,8,8,128]{3,2,1,0:T(8,128)S(1)} %fusion, f32[128,8]{1,0:T(8,128)S(1)} %copy.19, f32[128,8]{1,0:T(8,128)S(1)} %copy.9, bf16[128,256,128]{2,1,0:T(8,128)(2,1)S(1)} %bitcast.33, bf16[8,128,8,128]{3,2,0,1:T(8,128)(2,1)} %get-tuple-element.13, bf16[8,128,8,128]{3,2,0,1:T(8,128)(2,1)} %get-tuple-element.14), kind=kOutput, calls=%fused_computation.16 | convolution fusion | flops 549453824 | bytes 18882560 | tf_op jit(solution)/shard_map/crbk,rkn->crbn/dot_general | solution.py:45
  270.9 2.1 convert_element_type.11
  272.9 4.1 %copy.26 = bf16[2,4,128,1024]{3,2,1,0:T(8,128)(2,1)} copy(bf16[2,4,128,1024]{3,1,0,2:T(4,128)(2,1)} %convert_element_type.11) | data formatting | bytes 4194304 | tf_op jit(solution)/shard_map/convert_element_type | solution.py:49
  (4 shorter events, 0.0 us)
Async XLA Ops:
  6.5 192.5 %all-gather.2.cloned.1.call-start = ((), (), s32[]{:S(2)}) async-start(), calls=%async_computation | async-start | bytes 36208640 | tf_op jit(solution)/shard_map/all_gather | solution.py:33
  9.3 7.6 %collective-permute-start = (bf16[8,1,1024]{2,0,1:T(8,128)(2,1)S(1)}, bf16[8,1,1024]{2,0,1:T(8,128)(2,1)S(1)}, u32[]{:S(2)}, u32[]{:S(2)}) collective-permute-start(bf16[8,1,1024]{2,0,1:T(8,128)(2,1)S(1)} %get-tuple-element.5), channel_id=1, source_target_pairs={{0,1},{1,2},{2,3},{3,4},{4,5},{5,6},{6,7},{8,9},{9,10},{10,11},{11... | collective-permute-start | bytes 49160 | tf_op jit(solution)/shard_map/ppermute | solution.py:16
  15.6 6.0 %collective-permute-start.1 = (bf16[8,1,1024]{2,0,1:T(8,128)(2,1)S(1)}, bf16[8,1,1024]{2,0,1:T(8,128)(2,1)S(1)}, u32[]{:S(2)}, u32[]{:S(2)}) collective-permute-start(bf16[8,1,1024]{2,0,1:T(8,128)(2,1)S(1)} %get-tuple-element.6), channel_id=1, source_target_pairs={{1,0},{2,1},{3,2},{4,3},{5,4},{6,5},{7,6},{9,8},{10,9},{11,10},{12... | collective-permute-start | bytes 49160 | tf_op jit(solution)/shard_map/ppermute | solution.py:17
  23.2 0.7 copy-start.2
  23.2 0.7 copy-start.3
  23.2 1.5 copy-start.1
  258.6 3.5 %copy-start = (bf16[1024,8,128]{2,1,0:T(8,128)(2,1)S(1)}, bf16[1024,8,128]{2,1,0:T(8,128)(2,1)}, u32[]{:S(2)}) copy-start(bf16[1024,8,128]{2,1,0:T(8,128)(2,1)} %gather_fusion.1) | copy-start | bytes 6291460
  258.6 6.9 %slice-start = ((s8[8388608]{0:T(1024)(128)(4,1)}), s8[4194304]{0:T(1024)(128)(4,1)S(1)}, s32[]{:S(2)}) async-start(s8[8388608]{0:T(1024)(128)(4,1)} %bitcast.32), calls=%async_computation.1 | async-start | bytes 8388608
  262.2 3.3 %slice-start.1 = ((s8[8388608]{0:T(1024)(128)(4,1)}), s8[4194304]{0:T(1024)(128)(4,1)S(1)}, s32[]{:S(2)}) async-start(s8[8388608]{0:T(1024)(128)(4,1)} %bitcast.32), calls=%async_computation.2 | async-start | bytes 8388608
Sparse Core Ops, SparseCore 0:
  23.4 175.6 all-gather.1
where the time goes:
time: 285 us; the launch traced here: 284 us
  waiting for transfers between devices  179 us (63%)
  local copies, waits for them, and re-layouts  76.9 us (27%)
  between operations  13.5 us (5%)
  starting transfers between devices  7.62 us (3%)
  matrix products  5.36 us (2%)
    all_gather x1, waiting for transfers between devices, on_device(): window = lax.all_gather(rimmed, 'lon', axis=2, tiled=True)  174 us
    gather x2, local copies, waits for them, and re-layouts, on_device(): tiles[:, upper_rows, trailing]  19.7 us
    gather x2, local copies, waits for them, and re-layouts, on_device(): tiles[:, local_rows, trailing]  19.5 us
    gather x1, local copies, waits for them, and re-layouts, on_device(): tiles[:, upper_rows, leading]  16.2 us
    gather x1, local copies, waits for them, and re-layouts, on_device(): tiles[:, local_rows, leading]  11.1 us
    ppermute x1, starting transfers between devices, with_halo(): before = lax.ppermute(last, axis, up)  6.33 us
    convert_element_type x2, local copies, waits for them, and re-layouts, on_device(): return result.reshape(tracers.shape).astype(jnp.bfloat16)  6.13 us
  transfers between devices with their start and end apart: 3, of which 2 were waited for; matrix products, arithmetic and copies ran while one was open for 0% of the time, Pallas kernels for 0%

commit v1 on v0

v1 whole, which is shorter than its diff:
```python
import functools

import jax
import jax.numpy as jnp
from jax import lax
from jax.experimental import pallas as pl
from jax.experimental.pallas import tpu as pltpu
from jax.sharding import PartitionSpec as P

BLK = 128
LON = 16
LAT = 8
BLOCKS = 8
CH = 8
ROWS = 128
RIM = ROWS + 2
QROWS = 32
QSRC = QROWS + 2
POLAR = ((56, 17), (-25, 58), (-9, 26), (-9, 26))
POLAR_BASE = (0, 17, 75, 101)
PLAIN = ((-1, 10),) * 4
PLAIN_BASE = (0, 10, 20, 30)
SLOTS = 127
MESH = pl.DeviceIdType.MESH


def pieces(window):
    low, width = window
    out = []
    for dist in range(-4, 10):
        first = max(low, 8 * dist)
        last = min(low + width, 8 * dist + 8)
        if first < last:
            out.append((dist, first - 8 * dist, last - first, first - low))
    return out


def exchange_kernel(tracers, window, x, t32, halo_sem, send_sem, recv_sem, own_sem):
    lon = lax.axis_index("lon")
    lat = lax.axis_index("lat")
    north = lax.rem(lat + LAT - 1, LAT)
    south = lax.rem(lat + 1, LAT)

    def behind(dist):
        return lax.rem(lon - dist + LON, LON)

    barrier = pltpu.get_barrier_semaphore()
    for other in (north, south):
        pl.semaphore_signal(barrier, inc=1, device_id=(lon, other), device_id_type=MESH)
    polar_dists = sorted({s * p[0] % LON for w in POLAR for p in pieces(w) for s in (1, -1) if p[0]})
    plain_dists = sorted({s * p[0] % LON for w in PLAIN for p in pieces(w) for s in (1, -1) if p[0]})

    def greet(dists):
        for d in dists:
            pl.semaphore_signal(barrier, inc=1, device_id=(behind(d), lat), device_id_type=MESH)
        pl.semaphore_wait(barrier, len(dists) + 2)

    @pl.when(lat == 0)
    def _():
        greet(polar_dists)

    @pl.when(lat != 0)
    def _():
        greet(plain_dists)

    for g in range(BLOCKS):
        for rb in range(ROWS // 16):
            for ch in range(CH):
                part = tracers[ch, 16 * rb : 16 * rb + 16, BLK * g : BLK * (g + 1)].astype(jnp.float32)
                t32[g, pl.ds(8 + 128 * rb + ch, 16, stride=8), :] = part

    down = pltpu.make_async_remote_copy(
        src_ref=t32.at[:, pl.ds(8 * ROWS, 8), :], dst_ref=t32.at[:, pl.ds(0, 8), :],
        send_sem=halo_sem.at[0], recv_sem=halo_sem.at[1], device_id=(lon, south), device_id_type=MESH)
    up = pltpu.make_async_remote_copy(
        src_ref=t32.at[:, pl.ds(8, 8), :], dst_ref=t32.at[:, pl.ds(8 * RIM - 8, 8), :],
        send_sem=halo_sem.at[2], recv_sem=halo_sem.at[3], device_id=(lon, north), device_id_type=MESH)
    down.start()
    up.start()
    for g in range(BLOCKS):
        x[g, 16 : 8 * RIM - 16, :] = t32[g, 16 : 8 * RIM - 16, :].astype(jnp.bfloat16)
    down.wait()
    up.wait()
    for g in range(BLOCKS):
        x[g, 0:16, :] = t32[g, 0:16, :].astype(jnp.bfloat16)
        x[g, 8 * RIM - 16 : 8 * RIM, :] = t32[g, 8 * RIM - 16 : 8 * RIM, :].astype(jnp.bfloat16)

    def send(windows, bases):
        copies = []
        count = 0
        for q in range(4):
            for dist, first, blocks, slot in pieces(windows[q]):
                src = x.at[pl.ds(first, blocks), pl.ds(8 * QROWS * q, 8 * QSRC), :]
                dst = window.at[pl.ds(bases[q] + slot, blocks)]
                if dist:
                    copy = pltpu.make_async_remote_copy(
                        src_ref=src, dst_ref=dst, send_sem=send_sem.at[count], recv_sem=recv_sem.at[count],
                        device_id=(behind(dist), lat), device_id_type=MESH)
                    count += 1
                else:
                    copy = pltpu.make_async_copy(src, dst, own_sem.at[q])
                copy.start()
                copies.append(copy)
        for copy in copies:
            copy.wait()

    @pl.when(lat == 0)
    def _():
        send(POLAR, POLAR_BASE)

    @pl.when(lat != 0)
    def _():
        send(PLAIN, PLAIN_BASE)


def interpolate_kernel(lat_row, lon_offset, lat_weight, window, interp, out, held, o32, sems):
    step = pl.program_id(0)
    lat = lax.axis_index("lat")
    quarter = step // 2

    def fetch(q, base, width):
        return pltpu.make_async_copy(window.at[pl.ds(base, width)], held.at[pl.ds(base, width)], sems.at[q])

    for polar, windows, bases in ((True, POLAR, POLAR_BASE), (False, PLAIN, PLAIN_BASE)):
        @pl.when((step == 0) & ((lat == 0) == polar))
        def _(windows=windows, bases=bases):
            for q in range(4):
                fetch(q, bases[q], windows[q][1]).start()

        for q in range(4):
            @pl.when((step == 2 * q) & ((lat == 0) == polar))
            def _(q=q, windows=windows, bases=bases):
                fetch(q, bases[q], windows[q][1]).wait()

    def of_quarter(values):
        return jnp.where(quarter == 0, values[0], jnp.where(quarter == 1, values[1], jnp.where(quarter == 2, values[2], values[3])))

    shift = jnp.where(
        lat == 0,
        of_quarter([b - w[0] for b, w in zip(POLAR_BASE, POLAR)]),
        of_quarter([b - w[0] for b, w in zip(PLAIN_BASE, PLAIN)]),
    )
    first_row = lat * ROWS

    for pair in range(8):
        start = pl.multiple_of(lax.rem(step, 2) * 128 + 16 * pair, 16)
        for half in range(2):
            j = 2 * pair + half
            row = 16 * step + j
            lead, trail = [], []
            for b in range(BLOCKS):
                g = shift + lon_offset[row, b] + b
                lead.append(held[g, pl.ds(start, 32), :])
                trail.append(held[g + 1, pl.ds(start, 32), :])
            lhs = jnp.concatenate([jnp.concatenate(lead, axis=0), jnp.concatenate(trail, axis=0)], axis=1)
            prod = jnp.dot(lhs, interp[j], preferred_element_type=jnp.float32)
            for b in range(BLOCKS):
                w = lat_weight[row, b]
                back = lat_row[row, b] < first_row + row
                c0 = jnp.where(back, 1.0 - w, 0.0)
                c1 = jnp.where(back, w, 1.0 - w)
                c2 = jnp.where(back, 0.0, w)
                at = 32 * b + 8 * half
                o32[b, 8 * j : 8 * j + 8, :] = (
                    c0 * prod[at : at + 8] + c1 * prod[at + 8 : at + 16] + c2 * prod[at + 16 : at + 24]
                )
    for b in range(BLOCKS):
        for ch in range(CH):
            out[ch, :, BLK * b : BLK * (b + 1)] = o32[b, pl.ds(ch, 16, stride=8), :].astype(jnp.bfloat16)


def on_device(tracers, interp, lat_weight, lat_row, lon_offset):
    packed = tracers.reshape(CH, ROWS, BLOCKS * BLK)
    copies = sum(1 for w in POLAR for p in pieces(w) if p[0])
    vmem = pl.BlockSpec(memory_space=pltpu.VMEM)
    smem = pl.BlockSpec(memory_space=pltpu.SMEM)
    anywhere = pl.BlockSpec(memory_space=pl.ANY)
    window = pl.pallas_call(
        exchange_kernel,
        out_shape=jax.ShapeDtypeStruct((SLOTS, 8 * QSRC, BLK), jnp.bfloat16),
        in_specs=[vmem],
        out_specs=anywhere,
        scratch_shapes=[
            pltpu.VMEM((BLOCKS, 8 * RIM, BLK), jnp.bfloat16),
            pltpu.VMEM((BLOCKS, 8 * RIM, BLK), jnp.float32),
            pltpu.SemaphoreType.DMA((4,)),
            pltpu.SemaphoreType.DMA((copies,)),
            pltpu.SemaphoreType.DMA((copies,)),
            pltpu.SemaphoreType.DMA((4,)),
        ],
        compiler_params=pltpu.CompilerParams(collective_id=0, has_side_effects=True, vmem_limit_bytes=40 << 20),
        name="exchange",
    )(packed)
    result = pl.pallas_call(
        interpolate_kernel,
        out_shape=jax.ShapeDtypeStruct((CH, ROWS, BLOCKS * BLK), jnp.bfloat16),
        grid=(8,),
        in_specs=[smem, smem, smem, anywhere, pl.BlockSpec((16, 2 * BLK, BLK), lambda i: (i, 0, 0))],
        out_specs=pl.BlockSpec((CH, 16, BLOCKS * BLK), lambda i: (0, i, 0)),
        scratch_shapes=[
            pltpu.VMEM((SLOTS, 8 * QSRC, BLK), jnp.bfloat16),
            pltpu.VMEM((BLOCKS, 8 * 16, BLK), jnp.float32),
            pltpu.SemaphoreType.DMA((4,)),
        ],
        compiler_params=pltpu.CompilerParams(vmem_limit_bytes=40 << 20),
        name="interpolate",
    )(lat_row, lon_offset, lat_weight, window, interp)
    return result.reshape(tracers.shape)


def solution(mesh):
    return jax.shard_map(
        on_device,
        mesh=mesh,
        in_specs=(
            P(None, None, "lat", "lon"),
            P("lat", None, None),
            P("lat", "lon"),
            P("lat", "lon"),
            P("lat", "lon"),
        ),
        out_specs=P(None, None, "lat", "lon"),
        check_vma=False,
    )
```

time: 285 us -> 117 us (0.41)
  waiting for transfers between devices: 179 us -> 0 us
  Pallas kernels: 0 us -> 109 us
  local copies, waits for them, and re-layouts: 76.9 us -> 7.35 us
  between operations: 13.5 us -> 0.03 us
  starting transfers between devices: 7.62 us -> 0 us
  matrix products: 5.36 us -> 0 us
    all_gather x1 -> x0, waiting for transfers between devices: 174 us -> none  [on_device(): window = lax.all_gather(rimmed, 'lon', axis=2, tiled=True)]
    pallas_call x0 -> x2, Pallas kernels: none -> 109 us  [the longest x1 96.5 us: on_device(): pl.pallas_call(exchange_kernel, out_shape=jax.ShapeDtypeStruct((SLOTS, 8...]
    gather x6 -> x0, local copies, waits for them, and re-layouts: 66.4 us -> none  [the longest x2 19.7 us: on_device(): tiles[:, upper_rows, trailing]]
    ppermute x2 -> x0, starting transfers between devices: 7.62 us -> none  [the longest x1 6.33 us: with_halo(): before = lax.ppermute(last, axis, up)]
    unnamed x13 -> x9, local copies, waits for them, and re-layouts: 0.79 us -> 7.35 us
    convert_element_type x2 -> x0, local copies, waits for them, and re-layouts: 6.13 us -> none  [on_device(): return result.reshape(tracers.shape).astype(jnp.bfloat16)]
    dot_general x2 -> x0, matrix products: 5.36 us -> none  [the longest x1 3.93 us: on_device(): jnp.einsum('crbk,rkn->crbn', lower, interp, preferred_element_type=jnp.fl...]
    ppermute x2 -> x0, waiting for transfers between devices: 4.68 us -> none  [the longest x1 4.68 us: with_halo(): after = lax.ppermute(initial, axis, down)]
  transfers between devices with their start and end apart: 3 -> 0, of which waited for: 2 -> 0; matrix products, arithmetic and copies ran while one was open for 0% -> 0% of each run, Pallas kernels for 0% -> 0%
where the time goes in v1:
time: 117 us; the launch traced here: 116 us
  Pallas kernels  109 us (93%)
  local copies, waits for them, and re-layouts  7.35 us (6%)
    pallas_call x1, Pallas kernels, on_device(): pl.pallas_call(exchange_kernel, out_shape=jax.ShapeDtypeStruct((SLOTS, 8...  96.5 us
    pallas_call x1, Pallas kernels, on_device(): pl.pallas_call(interpolate_kernel, out_shape=jax.ShapeDtypeStruct((CH, RO...  12.6 us
    unnamed x9, local copies, waits for them, and re-layouts  7.35 us

profile of v1, /device:TPU:1, one launch (start us, length us, event | category | flops | bytes accessed | tf_op | source)
XLA Modules:
  0.0 116.5 jit_solution(11257417363581029642)
XLA Ops:
  0.0 0.8 copy.8.lat_weight
  0.8 0.8 copy.6.lat_row
  1.6 0.8 copy.7.lon_offset
  2.4 0.0 copy-start.2
  2.4 1.6 %copy-done.2 = bf16[2,4,128,1024]{3,2,1,0:T(8,128)(2,1)S(1)} copy-done((bf16[2,4,128,1024]{3,2,1,0:T(8,128)(2,1)S(1)}, bf16[2,4,128,1024]{3,2,1,0:T(8,128)(2,1)}, u32[]{:S(2)}) %copy-start.2) | copy-done | bytes 2097176
  4.0 0.0 copy-start.1
  4.0 96.5 %exchange.1.window = bf16[127,272,128]{2,1,0:T(8,128)(2,1)S(1)} custom-call(bf16[8,128,1024]{2,1,0:T(8,128)(2,1)S(1)} %bitcast.2), custom_call_target="tpu_custom_call" | custom-call | tf_op jit(solution)/shard_map/exchange/pallas_call | solution.py:178
  100.5 0.0 copy-start
  100.5 3.4 %copy-done = bf16[127,272,128]{2,1,0:T(8,128)(2,1)} copy-done((bf16[127,272,128]{2,1,0:T(8,128)(2,1)}, bf16[127,272,128]{2,1,0:T(8,128)(2,1)S(1)}, u32[]{:S(2)}) %copy-start) | copy-done | bytes 8843288
  103.9 0.0 copy-done.1
  103.9 12.6 %interpolate.1 = bf16[8,128,1024]{2,1,0:T(8,128)(2,1)} custom-call(s32[128,8]{1,0:T(8,128)S(1)} %copy.6.lat_row, s32[128,8]{1,0:T(8,128)S(1)} %copy.7.lon_offset, f32[128,8]{1,0:T(8,128)S(1)} %copy.8.lat_weight, bf16[127,272,128]{2,1,0:T(8,128)(2,1)} %copy-done, bf16[128,256,128]{2,1,0:T(8,128)(2,1)S(1)} %copy-done.1), custom_call_target="tpu_custom_call" | custom-call | tf_op jit(solution)/shard_map/interpolate/pallas_call | solution.py:194
Async XLA Ops:
  2.4 1.6 %copy-start.2 = (bf16[2,4,128,1024]{3,2,1,0:T(8,128)(2,1)S(1)}, bf16[2,4,128,1024]{3,2,1,0:T(8,128)(2,1)}, u32[]{:S(2)}) copy-start(bf16[2,4,128,1024]{3,2,1,0:T(8,128)(2,1)} %param.5) | copy-start | bytes 6291460
  4.0 99.9 %copy-start.1 = (bf16[128,256,128]{2,1,0:T(8,128)(2,1)S(1)}, bf16[128,256,128]{2,1,0:T(8,128)(2,1)}, u32[]{:S(2)}) copy-start(bf16[128,256,128]{2,1,0:T(8,128)(2,1)} %interp.1) | copy-start | bytes 25165828
  100.5 3.4 %copy-start = (bf16[127,272,128]{2,1,0:T(8,128)(2,1)}, bf16[127,272,128]{2,1,0:T(8,128)(2,1)S(1)}, u32[]{:S(2)}) copy-start(bf16[127,272,128]{2,1,0:T(8,128)(2,1)S(1)} %exchange.1.window) | copy-start | bytes 26529796

commit v2 on v0

v2 whole, which is shorter than its diff:
```python
import functools

import jax
import jax.numpy as jnp
from jax import lax
from jax.experimental import pallas as pl
from jax.experimental.pallas import tpu as pltpu
from jax.sharding import PartitionSpec as P

BLK = 128
LON = 16
LAT = 8
BLOCKS = 8
CH = 8
ROWS = 128
RIM = ROWS + 2
QROWS = 32
QSRC = QROWS + 2
TILE_ROWS = 8 * QSRC
POLAR_SHIFT = (-56, 25, 9, 9)
POLAR_OWN = (17, 25, 9, 9)
SLOTS = (25, 58, 26, 26)
SIDES = (("n", 2), ("s", 6))
CHUNKS_A = {"n": ((0, 2), (2, 2)), "s": ((4, 2), (6, 2))}
CHUNKS_C = {"n": ((0, 2), (2, 3)), "s": ((5, 2), (7, 2))}
SEMS = 160
RELAY = 40
MESH = pl.DeviceIdType.MESH


def fused_kernel(lat_row, lon_offset, lat_weight, tracers, interp, out,
                 tbuf, mats, t32, w0, w1, w2, w3, relay, o32, load_sem, halo_sem, send_sem, recv_sem):
    lon = lax.axis_index("lon")
    lat = lax.axis_index("lat")
    odd = lax.rem(lon, 2) == 1
    far_z = lax.rem(lax.div(lon, 2), 2) == 1
    inner = odd != far_z
    polar = lat == 0
    relays = (lat == SIDES[0][1]) | (lat == SIDES[1][1])
    wins = (w0, w1, w2, w3)

    def at(lat_index, dist):
        return (lax.rem(lon + dist + LON, LON), lat_index)

    def pick(if_odd, if_even):
        return jnp.where(odd, if_odd, if_even)

    north = lax.rem(lat + LAT - 1, LAT)
    south = lax.rem(lat + 1, LAT)
    sib = at(lat, pick(-1, 1))
    nb = at(lat, pick(1, -1))
    zdist = jnp.where(far_z, -2, 2)
    xdist = jnp.where(far_z, -4, 4)

    load_tracers = pltpu.make_async_copy(tracers, tbuf, load_sem.at[0])
    load_mats = pltpu.make_async_copy(interp, mats, load_sem.at[1])
    load_tracers.start()
    load_mats.start()

    barrier = pltpu.get_barrier_semaphore()

    def greet(devices):
        for d in devices:
            pl.semaphore_signal(barrier, inc=1, device_id=d, device_id_type=MESH)

    greet([(lon, north), (lon, south)])

    @pl.when(polar)
    def _():
        greet([sib, nb, at(lat, zdist), at(lat, 4), at(lat, -4), at(lat, pick(3, -3))] + [(lon, s) for _, s in SIDES])

    @pl.when(jnp.logical_not(polar))
    def _():
        greet([sib, nb])

    @pl.when(relays)
    def _():
        greet([at(0, 0), at(lat, 8), at(lat, pick(-7, 7))])

    load_tracers.wait()
    for g in range(BLOCKS):
        for rb in range(ROWS // 16):
            for ch in range(CH):
                part = tbuf[ch, 16 * rb : 16 * rb + 16, BLK * g : BLK * (g + 1)].astype(jnp.float32)
                t32[g, pl.ds(8 + 128 * rb + ch, 16, stride=8), :] = part

    @pl.when(polar)
    def _():
        pl.semaphore_wait(barrier, 10)

    @pl.when(relays)
    def _():
        pl.semaphore_wait(barrier, 7)

    @pl.when(jnp.logical_not(polar | relays))
    def _():
        pl.semaphore_wait(barrier, 4)

    down = pltpu.make_async_remote_copy(
        src_ref=t32.at[:, pl.ds(8 * ROWS, 8), :], dst_ref=t32.at[:, pl.ds(0, 8), :],
        send_sem=halo_sem.at[0], recv_sem=halo_sem.at[1], device_id=(lon, south), device_id_type=MESH)
    up = pltpu.make_async_remote_copy(
        src_ref=t32.at[:, pl.ds(8, 8), :], dst_ref=t32.at[:, pl.ds(8 * RIM - 8, 8), :],
        send_sem=halo_sem.at[2], recv_sem=halo_sem.at[3], device_id=(lon, north), device_id_type=MESH)
    down.start()
    up.start()

    def pack(q, low, high):
        own = jnp.where(polar, POLAR_OWN[q], 1)
        for g in range(BLOCKS):
            wins[q][own + g, low:high, :] = t32[g, 8 * QROWS * q + low : 8 * QROWS * q + high, :].astype(jnp.bfloat16)

    pack(1, 0, TILE_ROWS)
    pack(2, 0, TILE_ROWS)
    pack(0, 16, TILE_ROWS)
    pack(3, 0, TILE_ROWS - 16)
    down.wait()
    up.wait()
    pack(0, 0, 16)
    pack(3, TILE_ROWS - 16, TILE_ROWS)
    load_mats.wait()

    ids = {}
    sent = []

    def copy(name, src, dst, to):
        index = ids.setdefault(name, len(ids))
        assert index < SEMS, name
        return pltpu.make_async_remote_copy(
            src_ref=src, dst_ref=dst, send_sem=send_sem.at[index], recv_sem=recv_sem.at[index],
            device_id=to, device_id_type=MESH)

    def when(cond, body):
        if cond is None:
            body()
        else:
            pl.when(cond)(body)

    def put(name, src, dst, to, cond=None):
        when(cond, lambda: copy(name, src, dst, to).start())
        sent.append((cond, lambda: copy(name, src, dst, to).wait_send()))

    def got(name, dst, cond=None):
        when(cond, lambda: copy(name, dst, dst, sib).wait_recv())

    def all_sent():
        for cond, wait in sent:
            when(cond, wait)
        sent.clear()

    def span(ref, first, count):
        return ref.at[pl.ds(first, count)]

    def c_wins(q):
        return wins[q], f"c{q}"

    even = jnp.logical_not(odd)
    outer = jnp.logical_not(inner)
    compute = functools.partial(interpolate, lat_row, lon_offset, lat_weight, mats, out, o32, polar, lat * ROWS)

    @pl.when(polar)
    def _():
        put("b sib", span(w1, 25, 8), span(w1, pick(33, 17), 8), sib)
        for q in (2, 3):
            put(f"c{q} sib", span(wins[q], 9, 8), span(wins[q], pick(17, 1), 8), sib)
        for i in range(2):
            put(f"b z{i}", span(w1, 25 + 4 * i, 4), span(w1, jnp.where(far_z, 41, 9) + 4 * i, 4), at(lat, zdist))
        for i in range(2):
            for side, band in SIDES:
                first, count = CHUNKS_A[side][i]
                put(f"a up {side}{i}", span(w0, 17 + first, count), span(relay, 2 * i, count), at(band, 0))
        got("b sib", span(w1, pick(17, 33), 8))
        put("b far", span(w1, pick(24, 25), 9), span(w1, pick(0, 49), 9), at(lat, pick(3, -3)))
        for q in (2, 3):
            got(f"c{q} sib", span(wins[q], pick(1, 17), 8))
            for i in range(2):
                for side, band in SIDES:
                    first, count = CHUNKS_C[side][i]
                    put(f"c{q} up {side}{i}", span(wins[q], pick(8, 9) + first, count),
                        span(relay, 4 + 5 * (q - 2) + 2 * i, count), at(band, 0), inner if q == 2 else None)
        for i in range(2):
            mine = span(w1, jnp.where(far_z, 9, 41) + 4 * i, 4)
            got(f"b z{i}", mine)
            put(f"b x{i}", mine, span(w1, jnp.where(far_z, 41, 9) + 4 * i, 4), at(lat, xdist))
            if i == 0:
                put("c2 nb", span(w2, pick(8, 9), 9), span(w2, pick(0, 17), 9), nb, outer)
        for i in range(2):
            near = jnp.where(far_z, 9, 41) + 4 * i
            to = jnp.where(far_z, pick(17, 1), pick(49, 33)) + 4 * i
            put(f"b fz{i}", span(w1, near, 4), span(w1, to, 4), sib)

        for i in range(2):
            for side, band in SIDES:
                first, count = CHUNKS_A[side][i]
                got(f"a8 down {side}{i}", span(w0, 8 + first, count))
                put(f"a f {side}{i}", span(w0, 8 + first, count), span(w0, first, count), sib, even)
                if side == "n" and i == 0:
                    put("a one", span(w0, 8, 1), span(w0, 16, 1), sib, odd)
        for i in range(2):
            for side, band in SIDES:
                first, count = CHUNKS_A[side][i]
                got(f"a7 down {side}{i}", span(w0, first, count), even)
                got(f"a f {side}{i}", span(w0, first, count), odd)
        got("a9 down", span(w0, 16, 1), odd)
        got("a one", span(w0, 16, 1), even)
        compute(0, w0)

        def finish_c(q):
            for i in range(2):
                for side, band in SIDES:
                    first, count = CHUNKS_C[side][i]
                    got(f"c{q} down {side}{i}", span(wins[q], pick(17, 0) + first, count), inner if q == 2 else None)
            if q == 2:
                got("c2 nb", span(w2, pick(17, 0), 9), outer)
            put(f"c{q} one", span(wins[q], pick(17, 8), 1), span(wins[q], pick(25, 0), 1), sib)
            got(f"c{q} one", span(wins[q], pick(0, 25), 1))

        finish_c(2)
        compute(2, w2)
        for i in range(2):
            far = jnp.where(far_z, 41, 9) + 4 * i
            got(f"b x{i}", span(w1, far, 4))
            to = jnp.where(far_z, pick(49, 33), pick(17, 1)) + 4 * i
            put(f"b fx{i}", span(w1, far, 4), span(w1, to, 4), sib)
        got("b far", span(w1, pick(49, 0), 9))
        put("b one", span(w1, pick(49, 8), 1), span(w1, pick(57, 0), 1), sib)
        finish_c(3)
        compute(3, w3)
        for i in range(2):
            got(f"b fz{i}", span(w1, jnp.where(far_z, pick(1, 17), pick(33, 49)) + 4 * i, 4))
            got(f"b fx{i}", span(w1, jnp.where(far_z, pick(33, 49), pick(1, 17)) + 4 * i, 4))
        got("b one", span(w1, pick(0, 57), 1))
        compute(1, w1)
        all_sent()

    @pl.when(jnp.logical_not(polar))
    def _():
        for q in range(4):
            put(f"left {q}", span(wins[q], 1, 1), span(wins[q], 9, 1), at(lat, -1))
            put(f"right {q}", span(wins[q], 8, 1), span(wins[q], 0, 1), at(lat, 1))

        for side, band in SIDES:
            @pl.when(lat == band)
            def _(side=side, band=band):
                plain = list(sent)
                sent.clear()
                items = [("a", i) for i in range(2)] + [("c2", i) for i in range(2)] + [("c3", i) for i in range(2)]

                def place(kind, i):
                    if kind == "a":
                        return 2 * i, 14 + 2 * i, CHUNKS_A[side][i]
                    base = 4 + 5 * (int(kind[1]) - 2) + 2 * i
                    return base, base + 14, CHUNKS_C[side][i]

                def across(kind, i):
                    slot, over, (first, count) = place(kind, i)
                    cond = inner if kind == "c2" else None
                    got(f"{kind} up {side}{i}", span(relay, slot, count), cond)
                    if kind == "a":
                        put(f"a8 over {side}{i}", span(relay, slot, count), span(relay, over, count), at(lat, 8))
                        put(f"a7 over {side}{i}", span(relay, slot, count), span(relay, over + 14, count), at(lat, -7), odd)
                        if side == "n" and i == 0:
                            put("a9 over", span(relay, slot, 1), span(relay, 32, 1), at(lat, 7), even)
                    else:
                        put(f"{kind} over {side}{i}", span(relay, slot, count), span(relay, over, count), nb, cond)

                def back(kind, i):
                    slot, over, (first, count) = place(kind, i)
                    cond = inner if kind == "c2" else None
                    if kind == "a":
                        got(f"a8 over {side}{i}", span(relay, over, count))
                        put(f"a8 down {side}{i}", span(relay, over, count), span(w0, 8 + first, count), at(0, 0))
                        got(f"a7 over {side}{i}", span(relay, over + 14, count), even)
                        put(f"a7 down {side}{i}", span(relay, over + 14, count), span(w0, first, count), at(0, 0), even)
                        if side == "n" and i == 0:
                            got("a9 over", span(relay, 32, 1), odd)
                            put("a9 down", span(relay, 32, 1), span(w0, 16, 1), at(0, 0), odd)
                    else:
                        q = int(kind[1])
                        got(f"{kind} over {side}{i}", span(relay, over, count), cond)
                        put(f"{kind} down {side}{i}", span(relay, over, count),
                            span(wins[q], pick(17, 0) + first, count), at(0, 0), cond)

                for k in range(len(items) + 1):
                    if k < len(items):
                        across(*items[k])
                    if k >= 1:
                        back(*items[k - 1])
                all_sent()
                sent.extend(plain)

        for q in range(4):
            got(f"left {q}", span(wins[q], 9, 1))
            got(f"right {q}", span(wins[q], 0, 1))
        for q in range(4):
            compute(q, wins[q])
        all_sent()


def interpolate(lat_row, lon_offset, lat_weight, mats, out, o32, polar, first_row, q, window):
    shift = jnp.where(polar, POLAR_SHIFT[q], 1)
    for part in range(2):
        def pair_of_rows(pair, carry, part=part):
            start = pl.multiple_of(128 * part + 16 * pair, 16)
            for half in range(2):
                j = 2 * pair + half
                row = QROWS * q + 16 * part + j
                lead, trail = [], []
                for b in range(BLOCKS):
                    g = shift + lon_offset[b, row] + b
                    if q == 0:
                        g = jnp.maximum(g, 0)
                    lead.append(window[g, pl.ds(start, 32), :])
                    trail.append(window[g + 1, pl.ds(start, 32), :])
                lhs = jnp.concatenate([jnp.concatenate(lead, axis=0), jnp.concatenate(trail, axis=0)], axis=1)
                prod = jnp.dot(lhs, mats[row], preferred_element_type=jnp.float32)
                for b in range(BLOCKS):
                    w = lat_weight[b, row]
                    back = lat_row[b, row] < first_row + row
                    c0 = jnp.where(back, 1.0 - w, 0.0)
                    c1 = jnp.where(back, w, 1.0 - w)
                    c2 = jnp.where(back, 0.0, w)
                    at = 32 * b + 8 * half
                    o32[b, pl.ds(pl.multiple_of(8 * j, 8), 8), :] = (
                        c0 * prod[at : at + 8] + c1 * prod[at + 8 : at + 16] + c2 * prod[at + 16 : at + 24]
                    )
            return carry

        lax.fori_loop(0, 8, pair_of_rows, 0)
        low = QROWS * q + 16 * part
        for b in range(BLOCKS):
            for ch in range(CH):
                out[ch, low : low + 16, BLK * b : BLK * (b + 1)] = o32[b, pl.ds(ch, 16, stride=8), :].astype(jnp.bfloat16)


def on_device(tracers, interp, lat_weight, lat_row, lon_offset):
    packed = tracers.reshape(CH, ROWS, BLOCKS * BLK)
    smem = pl.BlockSpec(memory_space=pltpu.SMEM)
    anywhere = pl.BlockSpec(memory_space=pl.ANY)
    result = pl.pallas_call(
        fused_kernel,
        out_shape=jax.ShapeDtypeStruct((CH, ROWS, BLOCKS * BLK), jnp.bfloat16),
        in_specs=[smem, smem, smem, anywhere, anywhere],
        out_specs=pl.BlockSpec(memory_space=pltpu.VMEM),
        scratch_shapes=[
            pltpu.VMEM((CH, ROWS, BLOCKS * BLK), jnp.bfloat16),
            pltpu.VMEM((ROWS, 2 * BLK, BLK), jnp.bfloat16),
            pltpu.VMEM((BLOCKS, 8 * RIM, BLK), jnp.float32),
        ] + [pltpu.VMEM((n, TILE_ROWS, BLK), jnp.bfloat16) for n in SLOTS] + [
            pltpu.VMEM((RELAY, TILE_ROWS, BLK), jnp.bfloat16),
            pltpu.VMEM((BLOCKS, 8 * 16, BLK), jnp.float32),
            pltpu.SemaphoreType.DMA((2,)),
            pltpu.SemaphoreType.DMA((4,)),
            pltpu.SemaphoreType.DMA((SEMS,)),
            pltpu.SemaphoreType.DMA((SEMS,)),
        ],
        compiler_params=pltpu.CompilerParams(collective_id=0, has_side_effects=True, vmem_limit_bytes=56 << 20),
        name="advect",
    )(lat_row.T, lon_offset.T, lat_weight.T, packed, interp)
    return result.reshape(tracers.shape)


def solution(mesh):
    return jax.shard_map(
        on_device,
        mesh=mesh,
        in_specs=(
            P(None, None, "lat", "lon"),
            P("lat", None, None),
            P("lat", "lon"),
            P("lat", "lon"),
            P("lat", "lon"),
        ),
        out_specs=P(None, None, "lat", "lon"),
        check_vma=False,
    )
```

time: 285 us -> 66.6 us (0.23)
  the two profiles are of different devices: /device:TPU:1 before, /device:TPU:9 now
where the time goes in v2:
time: 66.6 us; the launch traced here: 66.4 us
  Pallas kernels  63.3 us (95%)
  local copies, waits for them, and re-layouts  3.08 us (5%)
    pallas_call x1, Pallas kernels, on_device(): pl.pallas_call(fused_kernel, out_shape=jax.ShapeDtypeStruct((CH, ROWS, BL...  63.3 us
    unnamed x1, local copies, waits for them, and re-layouts  3.08 us

profile of v2, /device:TPU:9, one launch (start us, length us, event | category | flops | bytes accessed | tf_op | source)
XLA Modules:
  0.0 66.4 jit_solution(12718476785797138716)
XLA Ops:
  0.0 63.3 %advect.1 = bf16[8,128,1024]{2,1,0:T(8,128)(2,1)} custom-call(s32[8,128]{1,0:T(8,128)} %bitcast.7, s32[8,128]{1,0:T(8,128)} %bitcast.8, f32[8,128]{1,0:T(8,128)} %bitcast.9, bf16[8,128,1024]{2,1,0:T(8,128)(2,1)} %bitcast.6, bf16[128,256,128]{2,1,0:T(8,128)(2,1)} %interp.1), custom_call_target="tpu_custom_call" | custom-call | tf_op jit(solution)/shard_map/advect/pallas_call | solution.py:340
  63.4 3.1 %copy.7 = bf16[2,4,128,1024]{3,2,1,0:T(8,128)(2,1)} copy(bf16[2,4,128,1024]{3,2,1,0:T(8,128)(2,1)} %bitcast.5) | data formatting | bytes 4194304

commit v3 on v2

v3 whole, which is shorter than its diff:
```python
import functools

import jax
import jax.numpy as jnp
from jax import lax
from jax.experimental import pallas as pl
from jax.experimental.pallas import tpu as pltpu
from jax.sharding import PartitionSpec as P

BLK = 128
LON = 16
LAT = 8
BLOCKS = 8
CH = 8
ROWS = 128
RIM = ROWS + 2
QROWS = 32
QSRC = QROWS + 2
TILE_ROWS = 8 * QSRC
POLAR_SHIFT = (-56, 25, 9, 9)
POLAR_OWN = (17, 25, 9, 9)
SLOTS = (25, 58, 26, 26)
SIDES = (("n", 2, (0, 2)), ("s", 6, (4, 6)))
SEMS = 128
RELAY = 16
MESH = pl.DeviceIdType.MESH


def fused_kernel(lat_row, lon_offset, lat_weight, tracers, interp, out,
                 tbuf, mats, t32, w0, w1, w2, w3, relay, o32, load_sem, halo_sem, send_sem, recv_sem):
    lon = lax.axis_index("lon")
    lat = lax.axis_index("lat")
    odd = lax.rem(lon, 2) == 1
    far_z = lax.rem(lax.div(lon, 2), 2) == 1
    inner = odd != far_z
    polar = lat == 0
    relays = (lat == SIDES[0][1]) | (lat == SIDES[1][1])
    wins = (w0, w1, w2, w3)

    def at(lat_index, dist):
        return (lax.rem(lon + dist + LON, LON), lat_index)

    def pick(if_odd, if_even):
        return jnp.where(odd, if_odd, if_even)

    north = lax.rem(lat + LAT - 1, LAT)
    south = lax.rem(lat + 1, LAT)
    sib = at(lat, pick(-1, 1))
    nb = at(lat, pick(1, -1))
    zdist = jnp.where(far_z, -2, 2)
    xdist = jnp.where(far_z, -4, 4)

    load_tracers = pltpu.make_async_copy(tracers, tbuf, load_sem.at[0])
    load_mats = pltpu.make_async_copy(interp, mats, load_sem.at[1])
    load_tracers.start()
    load_mats.start()

    barrier = pltpu.get_barrier_semaphore()
    even = jnp.logical_not(odd)
    outer = jnp.logical_not(inner)
    one = jnp.int32(1)
    none = jnp.int32(0)

    def greet(*devices):
        for d in devices:
            pl.semaphore_signal(barrier, inc=1, device_id=d, device_id_type=MESH)

    greet((lon, north), (lon, south))

    @pl.when(polar)
    def _():
        greet(sib, at(lat, zdist), at(lat, pick(2, -2)), at(lat, -xdist), at(lat, pick(4, -4)), at(lat, pick(3, -3)))
        pl.when(outer)(lambda: greet(nb))
        pl.when(odd)(lambda: greet(at(lat, 9)))
        for _, band, _ in SIDES:
            greet(at(band, 8), at(band, 0))
            pl.when(even)(lambda band=band: greet(at(band, jnp.where(far_z, 8, 4))))

    @pl.when(jnp.logical_not(polar))
    def _():
        greet(sib, nb)

    @pl.when(relays)
    def _():
        greet(at(0, 0), at(0, pick(1, -1)))
        pl.when(even)(lambda: greet(at(0, jnp.where(far_z, -1, 3))))

    load_tracers.wait()
    for g in range(BLOCKS):
        for rb in range(ROWS // 16):
            for ch in range(CH):
                part = tbuf[ch, 16 * rb : 16 * rb + 16, BLK * g : BLK * (g + 1)].astype(jnp.float32)
                t32[g, pl.ds(8 + 128 * rb + ch, 16, stride=8), :] = part

    def pack(q, low, high):
        own = jnp.where(polar, POLAR_OWN[q], 1)
        for g in range(BLOCKS):
            wins[q][own + g, low:high, :] = t32[g, 8 * QROWS * q + low : 8 * QROWS * q + high, :].astype(jnp.bfloat16)

    pack(1, 0, TILE_ROWS)
    pack(2, 0, TILE_ROWS)

    greeted = 4 + jnp.where(polar, 8 + jnp.where(outer, one, none) + jnp.where(even, one, 2 * one), none)
    greeted = greeted + jnp.where(relays, 2 + jnp.where(even, one, none), none)
    pl.semaphore_wait(barrier, greeted)

    down = pltpu.make_async_remote_copy(
        src_ref=t32.at[:, pl.ds(8 * ROWS, 8), :], dst_ref=t32.at[:, pl.ds(0, 8), :],
        send_sem=halo_sem.at[0], recv_sem=halo_sem.at[1], device_id=(lon, south), device_id_type=MESH)
    up = pltpu.make_async_remote_copy(
        src_ref=t32.at[:, pl.ds(8, 8), :], dst_ref=t32.at[:, pl.ds(8 * RIM - 8, 8), :],
        send_sem=halo_sem.at[2], recv_sem=halo_sem.at[3], device_id=(lon, north), device_id_type=MESH)
    down.start()
    up.start()

    ids = {}
    sent = []

    def copy(name, src, dst, to):
        index = ids.setdefault(name, len(ids))
        assert index < SEMS, name
        return pltpu.make_async_remote_copy(
            src_ref=src, dst_ref=dst, send_sem=send_sem.at[index], recv_sem=recv_sem.at[index],
            device_id=to, device_id_type=MESH)

    def when(cond, body):
        if cond is None:
            body()
        else:
            pl.when(cond)(body)

    def put(name, src, dst, to, cond=None):
        when(cond, lambda: copy(name, src, dst, to).start())
        sent.append((cond, lambda: copy(name, src, dst, to).wait_send()))

    def got(name, dst, cond=None):
        when(cond, lambda: copy(name, dst, dst, sib).wait_recv())

    def all_sent():
        for cond, wait in sent:
            when(cond, wait)
        sent.clear()

    def span(ref, first, count):
        return ref.at[pl.ds(first, count)]

    compute = functools.partial(interpolate, lat_row, lon_offset, lat_weight, mats, out, o32, polar, lat * ROWS)
    pairs = range(0, BLOCKS, 2)

    @pl.when(polar)
    def _():
        def up_c(q, cond=None):
            for i in range(2):
                for side, band, firsts in SIDES:
                    put(f"c{q} up {side}{i}", span(wins[q], 9 + firsts[i], 2), span(relay, 8 + 4 * (q - 2) + 2 * i, 2),
                        at(band, pick(1, -1)), cond)

        for i in pairs:
            put(f"b z{i}", span(w1, 25 + i, 2), span(w1, jnp.where(far_z, 41, 9) + i, 2), at(lat, zdist))
        up_c(2, inner)
        for i in range(0, BLOCKS, 4):
            put(f"b far{i}", span(w1, 25 + i, 4), span(w1, pick(1, 49) + i, 4), at(lat, pick(3, -3)))
        put("b end", span(w1, pick(25, 32), 1), span(w1, pick(57, 0), 1), at(lat, pick(-4, 4)))
        put("b sib", span(w1, 25, 8), span(w1, pick(33, 17), 8), sib)
        put("c2 sib", span(w2, 9, 8), span(w2, pick(17, 1), 8), sib)
        put("c2 end", span(w2, pick(9, 16), 1), span(w2, pick(25, 0), 1), at(lat, pick(-2, 2)))

        for g in range(BLOCKS):
            first = t32[g, 8:16, :]
            w0[17 + g, 0:16, :] = jnp.concatenate([jnp.zeros_like(first), first], axis=0).astype(jnp.bfloat16)
        pack(0, 16, TILE_ROWS)
        for i in range(2):
            for side, band, firsts in SIDES:
                put(f"a8 up {side}{i}", span(w0, 17 + firsts[i], 2), span(relay, 2 * i, 2), at(band, 0))
        for i in range(2):
            for side, band, firsts in SIDES:
                put(f"a7 up {side}{i}", span(w0, 17 + firsts[i], 2), span(relay, 4 + 2 * i, 2),
                    at(band, jnp.where(far_z, -3, 1)), odd)
        put("a9", span(w0, 17, 1), span(w0, 16, 1), at(lat, -9), even)

        pack(3, 0, TILE_ROWS - 16)
        down.wait()
        up.wait()
        pack(3, TILE_ROWS - 16, TILE_ROWS)
        up_c(3)
        put("c3 sib", span(w3, 9, 8), span(w3, pick(17, 1), 8), sib)
        put("c3 end", span(w3, pick(9, 16), 1), span(w3, pick(25, 0), 1), at(lat, pick(-2, 2)))

        for i in pairs:
            mine = span(w1, jnp.where(far_z, 9, 41) + i, 2)
            got(f"b z{i}", mine)
            put(f"b x{i}", mine, span(w1, jnp.where(far_z, 41, 9) + i, 2), at(lat, xdist))
            put(f"b fz{i}", mine, span(w1, jnp.where(far_z, pick(17, 1), pick(49, 33)) + i, 2), sib)
            if i == 0:
                for k in range(0, BLOCKS, 4):
                    put(f"c2 nb{k}", span(w2, 9 + k, 4), span(w2, pick(1, 17) + k, 4), nb, outer)

        load_mats.wait()

        def finish_c(q, cond=None):
            got(f"c{q} sib", span(wins[q], pick(1, 17), 8))
            got(f"c{q} end", span(wins[q], pick(25, 0), 1))
            for i in range(2):
                for side, _, firsts in SIDES:
                    got(f"c{q} down {side}{i}", span(wins[q], pick(17, 1) + firsts[i], 2), cond)
            if q == 2:
                for k in range(0, BLOCKS, 4):
                    got(f"c2 nb{k}", span(w2, pick(17, 1) + k, 4), outer)
            put(f"c{q} one", span(wins[q], pick(17, 8), 1), span(wins[q], pick(25, 0), 1), sib)
            got(f"c{q} one", span(wins[q], pick(0, 25), 1))

        finish_c(2, inner)
        compute(2, w2)

        for i in range(2):
            for side, _, firsts in SIDES:
                got(f"a8 down {side}{i}", span(w0, 8 + firsts[i], 2))
                put(f"a f {side}{i}", span(w0, 8 + firsts[i], 2), span(w0, firsts[i], 2), sib, even)
                if firsts[i] == 0:
                    put("a one", span(w0, 8, 1), span(w0, 16, 1), sib, odd)
        for i in range(2):
            for side, _, firsts in SIDES:
                got(f"a7 down {side}{i}", span(w0, firsts[i], 2), even)
                got(f"a f {side}{i}", span(w0, firsts[i], 2), odd)
        got("a9", span(w0, 16, 1), odd)
        got("a one", span(w0, 16, 1), even)
        compute(0, w0)

        for i in pairs:
            far = jnp.where(far_z, 41, 9) + i
            got(f"b x{i}", span(w1, far, 2))
            put(f"b fx{i}", span(w1, far, 2), span(w1, jnp.where(far_z, pick(49, 33), pick(17, 1)) + i, 2), sib)
        for i in range(0, BLOCKS, 4):
            got(f"b far{i}", span(w1, pick(49, 1) + i, 4))
        got("b end", span(w1, pick(57, 0), 1))
        put("b one", span(w1, pick(49, 8), 1), span(w1, pick(57, 0), 1), sib)
        finish_c(3)
        compute(3, w3)
        got("b sib", span(w1, pick(17, 33), 8))
        for i in pairs:
            got(f"b fz{i}", span(w1, jnp.where(far_z, pick(1, 17), pick(33, 49)) + i, 2))
            got(f"b fx{i}", span(w1, jnp.where(far_z, pick(33, 49), pick(1, 17)) + i, 2))
        got("b one", span(w1, pick(0, 57), 1))
        compute(1, w1)
        all_sent()

    @pl.when(jnp.logical_not(polar))
    def _():
        def sides(q):
            put(f"left {q}", span(wins[q], 1, 1), span(wins[q], 9, 1), at(lat, -1))
            put(f"right {q}", span(wins[q], 8, 1), span(wins[q], 0, 1), at(lat, 1))

        sides(1)
        sides(2)
        pack(0, 16, TILE_ROWS)
        pack(3, 0, TILE_ROWS - 16)
        down.wait()
        up.wait()
        pack(0, 0, 16)
        pack(3, TILE_ROWS - 16, TILE_ROWS)
        sides(0)
        sides(3)

        for side, band, firsts in SIDES:
            @pl.when(lat == band)
            def _(side=side, firsts=firsts):
                plain = list(sent)
                sent.clear()

                def pass_on(name, i, slot, win, first, dist, cond=None):
                    block = span(relay, slot + 2 * i, 2)
                    got(f"{name} up {side}{i}", block, cond)
                    put(f"{name} down {side}{i}", block, span(win, first + firsts[i], 2), at(0, dist), cond)

                for i in range(2):
                    pass_on("c2", i, 8, w2, pick(17, 1), 0, inner)
                for i in range(2):
                    pass_on("a8", i, 0, w0, 8, -8)
                for i in range(2):
                    pass_on("a7", i, 4, w0, 0, jnp.where(far_z, -8, -4), even)
                for i in range(2):
                    pass_on("c3", i, 12, w3, pick(17, 1), 0)
                all_sent()
                sent.extend(plain)

        load_mats.wait()
        for q in (1, 2, 0, 3):
            got(f"left {q}", span(wins[q], 9, 1))
            got(f"right {q}", span(wins[q], 0, 1))
            compute(q, wins[q])
        all_sent()


def interpolate(lat_row, lon_offset, lat_weight, mats, out, o32, polar, first_row, q, window):
    shift = jnp.where(polar, POLAR_SHIFT[q], 1)
    for part in range(2):
        def pair_of_rows(pair, carry, part=part):
            start = pl.multiple_of(128 * part + 16 * pair, 16)
            for half in range(2):
                j = 2 * pair + half
                row = QROWS * q + 16 * part + j
                lead, trail = [], []
                for b in range(BLOCKS):
                    g = shift + lon_offset[b, row] + b
                    if q == 0:
                        g = jnp.maximum(g, 0)
                    lead.append(window[g, pl.ds(start, 32), :])
                    trail.append(window[g + 1, pl.ds(start, 32), :])
                lhs = jnp.concatenate([jnp.concatenate(lead, axis=0), jnp.concatenate(trail, axis=0)], axis=1)
                prod = jnp.dot(lhs, mats[row], preferred_element_type=jnp.float32)
                for b in range(BLOCKS):
                    w = lat_weight[b, row]
                    back = lat_row[b, row] < first_row + row
                    c0 = jnp.where(back, 1.0 - w, 0.0)
                    c1 = jnp.where(back, w, 1.0 - w)
                    c2 = jnp.where(back, 0.0, w)
                    at = 32 * b + 8 * half
                    o32[b, pl.ds(pl.multiple_of(8 * j, 8), 8), :] = (
                        c0 * prod[at : at + 8] + c1 * prod[at + 8 : at + 16] + c2 * prod[at + 16 : at + 24]
                    )
            return carry

        lax.fori_loop(0, 8, pair_of_rows, 0)
        low = QROWS * q + 16 * part
        for b in range(BLOCKS):
            for ch in range(CH):
                out[ch, low : low + 16, BLK * b : BLK * (b + 1)] = o32[b, pl.ds(ch, 16, stride=8), :].astype(jnp.bfloat16)


def on_device(tracers, interp, lat_weight, lat_row, lon_offset):
    packed = tracers.reshape(CH, ROWS, BLOCKS * BLK)
    smem = pl.BlockSpec(memory_space=pltpu.SMEM)
    anywhere = pl.BlockSpec(memory_space=pl.ANY)
    result = pl.pallas_call(
        fused_kernel,
        out_shape=jax.ShapeDtypeStruct((CH, ROWS, BLOCKS * BLK), jnp.bfloat16),
        in_specs=[smem, smem, smem, anywhere, anywhere],
        out_specs=pl.BlockSpec(memory_space=pltpu.VMEM),
        scratch_shapes=[
            pltpu.VMEM((CH, ROWS, BLOCKS * BLK), jnp.bfloat16),
            pltpu.VMEM((ROWS, 2 * BLK, BLK), jnp.bfloat16),
            pltpu.VMEM((BLOCKS, 8 * RIM, BLK), jnp.float32),
        ] + [pltpu.VMEM((n, TILE_ROWS, BLK), jnp.bfloat16) for n in SLOTS] + [
            pltpu.VMEM((RELAY, TILE_ROWS, BLK), jnp.bfloat16),
            pltpu.VMEM((BLOCKS, 8 * 16, BLK), jnp.float32),
            pltpu.SemaphoreType.DMA((2,)),
            pltpu.SemaphoreType.DMA((4,)),
            pltpu.SemaphoreType.DMA((SEMS,)),
            pltpu.SemaphoreType.DMA((SEMS,)),
        ],
        compiler_params=pltpu.CompilerParams(collective_id=0, has_side_effects=True, vmem_limit_bytes=56 << 20),
        name="advect",
    )(lat_row.T, lon_offset.T, lat_weight.T, packed, interp)
    return result.reshape(tracers.shape)


def solution(mesh):
    return jax.shard_map(
        on_device,
        mesh=mesh,
        in_specs=(
            P(None, None, "lat", "lon"),
            P("lat", None, None),
            P("lat", "lon"),
            P("lat", "lon"),
            P("lat", "lon"),
        ),
        out_specs=P(None, None, "lat", "lon"),
        check_vma=False,
    )
```

time: 66.6 us -> 58.7 us (0.88)
  the two profiles are of different devices: /device:TPU:9 before, /device:TPU:1 now
where the time goes in v3:
time: 58.7 us; the launch traced here: 58.5 us
  Pallas kernels  55.4 us (94%)
  local copies, waits for them, and re-layouts  3.08 us (5%)
    pallas_call x1, Pallas kernels, on_device(): pl.pallas_call(fused_kernel, out_shape=jax.ShapeDtypeStruct((CH, ROWS, BL...  55.4 us
    unnamed x1, local copies, waits for them, and re-layouts  3.08 us

profile of v3, /device:TPU:1, one launch (start us, length us, event | category | flops | bytes accessed | tf_op | source)
XLA Modules:
  0.0 58.5 jit_solution(16228267672956996710)
XLA Ops:
  0.0 55.4 %advect.1 = bf16[8,128,1024]{2,1,0:T(8,128)(2,1)} custom-call(s32[8,128]{1,0:T(8,128)} %bitcast.7, s32[8,128]{1,0:T(8,128)} %bitcast.8, f32[8,128]{1,0:T(8,128)} %bitcast.9, bf16[8,128,1024]{2,1,0:T(8,128)(2,1)} %bitcast.6, bf16[128,256,128]{2,1,0:T(8,128)(2,1)} %interp.1), custom_call_target="tpu_custom_call" | custom-call | tf_op jit(solution)/shard_map/advect/pallas_call | solution.py:334
  55.4 3.1 %copy.7 = bf16[2,4,128,1024]{3,2,1,0:T(8,128)(2,1)} copy(bf16[2,4,128,1024]{3,2,1,0:T(8,128)(2,1)} %bitcast.5) | data formatting | bytes 4194304

commit v4 on v3

v4 whole, which is shorter than its diff:
```python
import functools

import jax
import jax.numpy as jnp
from jax import lax
from jax.experimental import pallas as pl
from jax.experimental.pallas import tpu as pltpu
from jax.sharding import PartitionSpec as P

BLK = 128
LON = 16
LAT = 8
BLOCKS = 8
CH = 8
ROWS = 128
RIM = ROWS + 2
QROWS = 32
QSRC = QROWS + 2
TILE_ROWS = 8 * QSRC
POLAR_SHIFT = (-56, 25, 9, 9)
POLAR_OWN = (17, 25, 9, 9)
SLOTS = (25, 58, 26, 26)
SIDES = (("n", 2, (0, 2)), ("s", 6, (4, 6)))
SEMS = 128
RELAY = 16
MESH = pl.DeviceIdType.MESH


def fused_kernel(lat_row_in, lon_offset_in, lat_weight_in, tracers, interp, out,
                 lat_row, lon_offset, lat_weight, tbuf, mats, t32, w0, w1, w2, w3, relay, o32, load_sem, halo_sem, send_sem, recv_sem):
    lon = lax.axis_index("lon")
    lat = lax.axis_index("lat")
    odd = lax.rem(lon, 2) == 1
    far_z = lax.rem(lax.div(lon, 2), 2) == 1
    inner = odd != far_z
    polar = lat == 0
    relays = (lat == SIDES[0][1]) | (lat == SIDES[1][1])
    wins = (w0, w1, w2, w3)

    def at(lat_index, dist):
        return (lax.rem(lon + dist + LON, LON), lat_index)

    def pick(if_odd, if_even):
        return jnp.where(odd, if_odd, if_even)

    north = lax.rem(lat + LAT - 1, LAT)
    south = lax.rem(lat + 1, LAT)
    sib = at(lat, pick(-1, 1))
    nb = at(lat, pick(1, -1))
    zdist = jnp.where(far_z, -2, 2)
    xdist = jnp.where(far_z, -4, 4)

    load_tracers = pltpu.make_async_copy(tracers, tbuf, load_sem.at[0])
    load_tracers.start()
    loads = [
        pltpu.make_async_copy(src, dst, load_sem.at[1 + i])
        for i, (src, dst) in enumerate(
            ((interp, mats), (lat_row_in, lat_row), (lon_offset_in, lon_offset), (lat_weight_in, lat_weight)))
    ]

    barrier = pltpu.get_barrier_semaphore()
    even = jnp.logical_not(odd)
    outer = jnp.logical_not(inner)
    one = jnp.int32(1)
    none = jnp.int32(0)

    def greet(*devices):
        for d in devices:
            pl.semaphore_signal(barrier, inc=1, device_id=d, device_id_type=MESH)

    greet((lon, north), (lon, south))

    @pl.when(polar)
    def _():
        greet(sib, at(lat, zdist), at(lat, pick(2, -2)), at(lat, -xdist), at(lat, pick(4, -4)), at(1, pick(3, -3) + zdist))
        pl.when(outer)(lambda: greet(nb))
        pl.when(odd)(lambda: greet(at(lat, 9)))
        for _, band, _ in SIDES:
            greet(at(band, 8), at(band, 0))
            pl.when(even)(lambda band=band: greet(at(band, jnp.where(far_z, 8, 4))))

    @pl.when(jnp.logical_not(polar))
    def _():
        greet(sib, nb)

    @pl.when(relays)
    def _():
        greet(at(0, 0), at(0, pick(1, -1)))
        pl.when(even)(lambda: greet(at(0, jnp.where(far_z, -1, 3))))

    @pl.when(lat == 1)
    def _():
        greet(at(0, zdist))

    for load in loads:
        load.start()
    load_tracers.wait()
    for g in range(BLOCKS):
        for rb in range(ROWS // 16):
            for ch in range(CH):
                part = tbuf[ch, 16 * rb : 16 * rb + 16, BLK * g : BLK * (g + 1)].astype(jnp.float32)
                t32[g, pl.ds(8 + 128 * rb + ch, 16, stride=8), :] = part

    def pack(q, low, high):
        own = jnp.where(polar, POLAR_OWN[q], 1)
        for g in range(BLOCKS):
            wins[q][own + g, low:high, :] = t32[g, 8 * QROWS * q + low : 8 * QROWS * q + high, :].astype(jnp.bfloat16)

    pack(1, 0, TILE_ROWS)
    pack(2, 0, TILE_ROWS)

    greeted = 4 + jnp.where(polar, 8 + jnp.where(outer, one, none) + jnp.where(even, one, 2 * one), none)
    greeted = greeted + jnp.where(lat == 1, one, none) + jnp.where(relays, 2 + jnp.where(even, one, none), none)
    pl.semaphore_wait(barrier, greeted)

    down = pltpu.make_async_remote_copy(
        src_ref=t32.at[:, pl.ds(8 * ROWS, 8), :], dst_ref=t32.at[:, pl.ds(0, 8), :],
        send_sem=halo_sem.at[0], recv_sem=halo_sem.at[1], device_id=(lon, south), device_id_type=MESH)
    up = pltpu.make_async_remote_copy(
        src_ref=t32.at[:, pl.ds(8, 8), :], dst_ref=t32.at[:, pl.ds(8 * RIM - 8, 8), :],
        send_sem=halo_sem.at[2], recv_sem=halo_sem.at[3], device_id=(lon, north), device_id_type=MESH)
    down.start()
    up.start()

    ids = {}
    sent = []

    def copy(name, src, dst, to):
        index = ids.setdefault(name, len(ids))
        assert index < SEMS, name
        return pltpu.make_async_remote_copy(
            src_ref=src, dst_ref=dst, send_sem=send_sem.at[index], recv_sem=recv_sem.at[index],
            device_id=to, device_id_type=MESH)

    def when(cond, body):
        if cond is None:
            body()
        else:
            pl.when(cond)(body)

    def span(ref, first, count):
        return ref, first, count

    def block_of(slots):
        ref, first, count = slots
        return ref.at[pl.ds(first, count)]

    def put(name, src, dst, to, cond=None):
        when(cond, lambda: copy(name, block_of(src), block_of(dst), to).start())
        sent.append((name, src[0], src[2], cond))

    def got(name, dst, cond=None):
        when(cond, lambda: copy(name, block_of(dst), block_of(dst), sib).wait_recv())

    def all_sent():
        for name, ref, count, cond in sent:
            block = ref.at[pl.ds(0, count)]
            when(cond, lambda: copy(name, block, block, sib).wait_send())
        sent.clear()

    compute = functools.partial(interpolate, lat_row, lon_offset, lat_weight, mats, out, o32, polar, lat * ROWS)
    pairs = range(0, BLOCKS, 2)

    def finish_c(q, cond=None):
        got(f"c{q} sib", span(wins[q], pick(1, 17), 8))
        got(f"c{q} end", span(wins[q], pick(25, 0), 1))
        for i in range(2):
            for side, _, firsts in SIDES:
                got(f"c{q} down {side}{i}", span(wins[q], pick(17, 1) + firsts[i], 2), cond)
        if q == 2:
            for k in range(0, BLOCKS, 4):
                got(f"c2 nb{k}", span(w2, pick(17, 1) + k, 4), outer)
        put(f"c{q} one", span(wins[q], pick(17, 8), 1), span(wins[q], pick(25, 0), 1), sib)
        got(f"c{q} one", span(wins[q], pick(0, 25), 1))

    @pl.when(polar)
    def _():
        def up_c(q, cond=None):
            for i in range(2):
                for side, band, firsts in SIDES:
                    put(f"c{q} up {side}{i}", span(wins[q], 9 + firsts[i], 2), span(relay, 8 + 4 * (q - 2) + 2 * i, 2),
                        at(band, pick(1, -1)), cond)

        for i in pairs:
            put(f"b z{i}", span(w1, 25 + i, 2), span(w1, jnp.where(far_z, 41, 9) + i, 2), at(lat, zdist))
        up_c(2, inner)
        for i in range(0, BLOCKS, 4):
            put(f"b far{i} out", span(w1, 25 + i, 4), span(relay, i, 4), at(1, zdist))
        put("b end", span(w1, pick(25, 32), 1), span(w1, pick(57, 0), 1), at(lat, pick(-4, 4)))
        put("b sib", span(w1, 25, 8), span(w1, pick(33, 17), 8), sib)
        put("c2 sib", span(w2, 9, 8), span(w2, pick(17, 1), 8), sib)
        put("c2 end", span(w2, pick(9, 16), 1), span(w2, pick(25, 0), 1), at(lat, pick(-2, 2)))

        for g in range(BLOCKS):
            first = t32[g, 8:16, :]
            w0[17 + g, 0:16, :] = jnp.concatenate([jnp.zeros_like(first), first], axis=0).astype(jnp.bfloat16)
        pack(0, 16, TILE_ROWS)
        for i in range(2):
            for side, band, firsts in SIDES:
                put(f"a8 up {side}{i}", span(w0, 17 + firsts[i], 2), span(relay, 2 * i, 2), at(band, 0))
        for i in range(2):
            for side, band, firsts in SIDES:
                put(f"a7 up {side}{i}", span(w0, 17 + firsts[i], 2), span(relay, 4 + 2 * i, 2),
                    at(band, jnp.where(far_z, -3, 1)), odd)
        put("a9", span(w0, 17, 1), span(w0, 16, 1), at(lat, -9), even)

        pack(3, 0, TILE_ROWS - 16)
        down.wait()
        up.wait()
        pack(3, TILE_ROWS - 16, TILE_ROWS)
        up_c(3)
        put("c3 sib", span(w3, 9, 8), span(w3, pick(17, 1), 8), sib)
        put("c3 end", span(w3, pick(9, 16), 1), span(w3, pick(25, 0), 1), at(lat, pick(-2, 2)))

        for i in pairs:
            mine = span(w1, jnp.where(far_z, 9, 41) + i, 2)
            got(f"b z{i}", mine)
            put(f"b x{i}", mine, span(w1, jnp.where(far_z, 41, 9) + i, 2), at(lat, xdist))
            put(f"b fz{i}", mine, span(w1, jnp.where(far_z, pick(17, 1), pick(49, 33)) + i, 2), sib)
            if i == 0:
                for k in range(0, BLOCKS, 4):
                    put(f"c2 nb{k}", span(w2, 9 + k, 4), span(w2, pick(1, 17) + k, 4), nb, outer)
        finish_c(2, inner)

    polar_sent = list(sent)
    sent.clear()

    @pl.when(jnp.logical_not(polar))
    def _():
        def sides(q):
            put(f"left {q}", span(wins[q], 1, 1), span(wins[q], 9, 1), at(lat, -1))
            put(f"right {q}", span(wins[q], 8, 1), span(wins[q], 0, 1), at(lat, 1))

        sides(1)
        sides(2)
        pack(0, 16, TILE_ROWS)
        pack(3, 0, TILE_ROWS - 16)
        down.wait()
        up.wait()
        pack(0, 0, 16)
        pack(3, TILE_ROWS - 16, TILE_ROWS)
        sides(0)
        sides(3)

        @pl.when(lat == 1)
        def _():
            plain = list(sent)
            sent.clear()
            for i in range(0, BLOCKS, 4):
                block = span(relay, i, 4)
                got(f"b far{i} out", block)
                put(f"b far{i}", block, span(w1, pick(1, 49) + i, 4), at(0, zdist + pick(3, -3)))
            all_sent()
            sent.extend(plain)

        for side, band, firsts in SIDES:
            @pl.when(lat == band)
            def _(side=side, firsts=firsts):
                plain = list(sent)
                sent.clear()

                def pass_on(name, i, slot, win, first, dist, cond=None):
                    block = span(relay, slot + 2 * i, 2)
                    got(f"{name} up {side}{i}", block, cond)
                    put(f"{name} down {side}{i}", block, span(win, first + firsts[i], 2), at(0, dist), cond)

                for i in range(2):
                    pass_on("c2", i, 8, w2, pick(17, 1), 0, inner)
                for i in range(2):
                    pass_on("a8", i, 0, w0, 8, -8)
                for i in range(2):
                    pass_on("a7", i, 4, w0, 0, jnp.where(far_z, -8, -4), even)
                for i in range(2):
                    pass_on("c3", i, 12, w3, pick(17, 1), 0)
                all_sent()
                sent.extend(plain)

        for q in range(4):
            got(f"left {q}", span(wins[q], 9, 1))
            got(f"right {q}", span(wins[q], 0, 1))

    plain_sent = list(sent)
    sent.clear()
    sent.extend(polar_sent)

    for load in loads:
        load.wait()
    compute(2, w2)

    @pl.when(polar)
    def _():
        for i in range(2):
            for side, _, firsts in SIDES:
                got(f"a8 down {side}{i}", span(w0, 8 + firsts[i], 2))
                put(f"a f {side}{i}", span(w0, 8 + firsts[i], 2), span(w0, firsts[i], 2), sib, even)
                if firsts[i] == 0:
                    put("a one", span(w0, 8, 1), span(w0, 16, 1), sib, odd)
        for i in range(2):
            for side, _, firsts in SIDES:
                got(f"a7 down {side}{i}", span(w0, firsts[i], 2), even)
                got(f"a f {side}{i}", span(w0, firsts[i], 2), odd)
        got("a9", span(w0, 16, 1), odd)
        got("a one", span(w0, 16, 1), even)

    compute(0, w0)

    @pl.when(polar)
    def _():
        for i in pairs:
            far = jnp.where(far_z, 41, 9) + i
            got(f"b x{i}", span(w1, far, 2))
            put(f"b fx{i}", span(w1, far, 2), span(w1, jnp.where(far_z, pick(49, 33), pick(17, 1)) + i, 2), sib)
        for i in range(0, BLOCKS, 4):
            got(f"b far{i}", span(w1, pick(49, 1) + i, 4))
        got("b end", span(w1, pick(57, 0), 1))
        put("b one", span(w1, pick(49, 8), 1), span(w1, pick(57, 0), 1), sib)
        finish_c(3)

    compute(3, w3)

    @pl.when(polar)
    def _():
        got("b sib", span(w1, pick(17, 33), 8))
        for i in pairs:
            got(f"b fz{i}", span(w1, jnp.where(far_z, pick(1, 17), pick(33, 49)) + i, 2))
            got(f"b fx{i}", span(w1, jnp.where(far_z, pick(33, 49), pick(1, 17)) + i, 2))
        got("b one", span(w1, pick(0, 57), 1))

    compute(1, w1)

    @pl.when(polar)
    def _():
        all_sent()

    sent.extend(plain_sent)

    @pl.when(jnp.logical_not(polar))
    def _():
        all_sent()


def interpolate(lat_row, lon_offset, lat_weight, mats, out, o32, polar, first_row, q, window):
    shift = jnp.where(polar, POLAR_SHIFT[q], 1)
    sublane = lax.broadcasted_iota(jnp.int32, (16, BLK), 0)

    def part_of_rows(part, carry):
        for j in range(16):
            start = pl.multiple_of(128 * part + 16 * (j // 2), 16)
            row = QROWS * q + 16 * part + j
            lead, trail, backs = [], [], []
            for b in range(BLOCKS):
                g = shift + lon_offset[b, row] + b
                if q == 0:
                    g = jnp.maximum(g, 0)
                back = lat_row[b, row] < first_row + row
                backs.append(back)
                if j % 2 == 0:
                    lower = sublane < jnp.where(back, 0, 8)
                else:
                    lower = sublane < jnp.where(back, 8, 16)
                for tiles, slot in ((lead, g), (trail, g + 1)):
                    tiles.append(jnp.where(lower, window[slot, pl.ds(start + 16, 16), :], window[slot, pl.ds(start, 16), :]))
            lhs = jnp.concatenate([jnp.concatenate(lead, axis=0), jnp.concatenate(trail, axis=0)], axis=1)
            prod = jnp.dot(lhs, mats[row], preferred_element_type=jnp.float32)
            for b in range(BLOCKS):
                w = lat_weight[b, row]
                first_south = backs[b] if j % 2 == 0 else jnp.logical_not(backs[b])
                c0 = jnp.where(first_south, 1.0 - w, w)
                c1 = jnp.where(first_south, w, 1.0 - w)
                o32[b, 8 * j : 8 * j + 8, :] = c0 * prod[16 * b : 16 * b + 8] + c1 * prod[16 * b + 8 : 16 * b + 16]
        low = pl.multiple_of(QROWS * q + 16 * part, 16)
        for b in range(BLOCKS):
            for ch in range(CH):
                out[ch, pl.ds(low, 16), BLK * b : BLK * (b + 1)] = o32[b, pl.ds(ch, 16, stride=8), :].astype(jnp.bfloat16)
        return carry

    lax.fori_loop(0, 2, part_of_rows, 0)


def store_kernel(src, dst, sem):
    copy = pltpu.make_async_copy(src, dst, sem)
    copy.start()
    copy.wait()


def on_device(tracers, interp, lat_weight, lat_row, lon_offset):
    packed = tracers.reshape(CH, ROWS, BLOCKS * BLK)
    anywhere = pl.BlockSpec(memory_space=pl.ANY)
    result = pl.pallas_call(
        fused_kernel,
        out_shape=pltpu.VMEM((CH, ROWS, BLOCKS * BLK), jnp.bfloat16),
        in_specs=[anywhere] * 5,
        out_specs=pl.BlockSpec(memory_space=pltpu.VMEM),
        scratch_shapes=[
            pltpu.SMEM((BLOCKS, ROWS), jnp.int32),
            pltpu.SMEM((BLOCKS, ROWS), jnp.int32),
            pltpu.SMEM((BLOCKS, ROWS), jnp.float32),
            pltpu.VMEM((CH, ROWS, BLOCKS * BLK), jnp.bfloat16),
            pltpu.VMEM((ROWS, 2 * BLK, BLK), jnp.bfloat16),
            pltpu.VMEM((BLOCKS, 8 * RIM, BLK), jnp.float32),
        ] + [pltpu.VMEM((n, TILE_ROWS, BLK), jnp.bfloat16) for n in SLOTS] + [
            pltpu.VMEM((RELAY, TILE_ROWS, BLK), jnp.bfloat16),
            pltpu.VMEM((BLOCKS, 8 * 16, BLK), jnp.float32),
            pltpu.SemaphoreType.DMA((5,)),
            pltpu.SemaphoreType.DMA((4,)),
            pltpu.SemaphoreType.DMA((SEMS,)),
            pltpu.SemaphoreType.DMA((SEMS,)),
        ],
        compiler_params=pltpu.CompilerParams(collective_id=0, has_side_effects=True, vmem_limit_bytes=56 << 20),
        name="advect",
    )(lat_row.T, lon_offset.T, lat_weight.T, packed, interp)
    stored = pl.pallas_call(
        store_kernel,
        out_shape=jax.ShapeDtypeStruct((CH, ROWS, BLOCKS * BLK), jnp.bfloat16),
        in_specs=[pl.BlockSpec(memory_space=pltpu.VMEM)],
        out_specs=anywhere,
        scratch_shapes=[pltpu.SemaphoreType.DMA],
        name="store",
    )(result)
    return stored.reshape(tracers.shape)


def solution(mesh):
    return jax.shard_map(
        on_device,
        mesh=mesh,
        in_specs=(
            P(None, None, "lat", "lon"),
            P("lat", None, None),
            P("lat", "lon"),
            P("lat", "lon"),
            P("lat", "lon"),
        ),
        out_specs=P(None, None, "lat", "lon"),
        check_vma=False,
    )
```

time: 58.7 us -> 51.9 us (0.88)
  Pallas kernels: 55.4 us -> 50 us
  local copies, waits for them, and re-layouts: 3.08 us -> 1.34 us
    pallas_call x1 -> x2, Pallas kernels: 55.4 us -> 50 us  [the longest x1 47 us: on_device(): pl.pallas_call(fused_kernel, out_shape=pltpu.VMEM((CH, ROWS, BLOCKS * BLK...]
    unnamed x1 -> x2, local copies, waits for them, and re-layouts: 3.08 us -> 1.34 us
where the time goes in v4:
time: 51.9 us; the launch traced here: 51.3 us
  Pallas kernels  50 us (96%)
  local copies, waits for them, and re-layouts  1.34 us (3%)
    pallas_call x1, Pallas kernels, on_device(): pl.pallas_call(fused_kernel, out_shape=pltpu.VMEM((CH, ROWS, BLOCKS * BLK...  47 us
    pallas_call x1, Pallas kernels, on_device(): pl.pallas_call(store_kernel, out_shape=jax.ShapeDtypeStruct((CH, ROWS, BL...  2.92 us
    unnamed x2, local copies, waits for them, and re-layouts  1.34 us

profile of v4, /device:TPU:1, one launch (start us, length us, event | category | flops | bytes accessed | tf_op | source)
XLA Modules:
  0.0 51.3 jit_solution(872877922903764262)
XLA Ops:
  0.0 47.0 %advect.1.src = bf16[8,128,1024]{2,1,0:T(8,128)(2,1)S(1)} custom-call(s32[8,128]{1,0:T(8,128)} %bitcast.6, s32[8,128]{1,0:T(8,128)} %bitcast.7, f32[8,128]{1,0:T(8,128)} %bitcast.8, bf16[8,128,1024]{2,1,0:T(8,128)(2,1)} %bitcast.5, bf16[128,256,128]{2,1,0:T(8,128)(2,1)} %interp.1), custom_call_target="tpu_custom_call" | custom-call | tf_op jit(solution)/shard_map/advect/pallas_call | solution.py:389
  47.1 0.0 copy-start
  47.1 1.3 %copy-done = bf16[8,128,1024]{2,1,0:T(8,128)(2,1)} copy-done((bf16[8,128,1024]{2,1,0:T(8,128)(2,1)}, bf16[8,128,1024]{2,1,0:T(8,128)(2,1)S(1)}, u32[]{:S(2)}) %copy-start) | copy-done | bytes 2097176
  48.4 2.9 %store.1 = bf16[8,128,1024]{2,1,0:T(8,128)(2,1)} custom-call(bf16[8,128,1024]{2,1,0:T(8,128)(2,1)} %copy-done), custom_call_target="tpu_custom_call" | custom-call | tf_op jit(solution)/shard_map/store/pallas_call | solution.py:412
Async XLA Ops:
  47.1 1.3 %copy-start = (bf16[8,128,1024]{2,1,0:T(8,128)(2,1)}, bf16[8,128,1024]{2,1,0:T(8,128)(2,1)S(1)}, u32[]{:S(2)}) copy-start(bf16[8,128,1024]{2,1,0:T(8,128)(2,1)S(1)} %advect.1.src) | copy-start | bytes 6291460

commit v5 on v4

v5 whole, which is shorter than its diff:
```python
import functools

import jax
import jax.numpy as jnp
from jax import lax
from jax.experimental import pallas as pl
from jax.experimental.pallas import tpu as pltpu
from jax.sharding import PartitionSpec as P

BLK = 128
LON = 16
LAT = 8
BLOCKS = 8
CH = 8
ROWS = 128
RIM = ROWS + 2
QROWS = 32
QSRC = QROWS + 2
TILE_ROWS = 8 * QSRC
POLAR_SHIFT = (-56, 25, 9, 9)
POLAR_OWN = (17, 25, 9, 9)
SLOTS = (25, 58, 26, 26)
SIDES = (("n", 2, (0, 2)), ("s", 6, (4, 6)))
PIECES = (("x", 0, 0, 4, 0), ("n", 2, 4, 1, 0), ("s", 6, 5, 1, 0), ("z", 1, 6, 2, 8))
SEMS = 128
RELAY = 16
MESH = pl.DeviceIdType.MESH


def fused_kernel(lat_row_in, lon_offset_in, lat_weight_in, tracers, interp, out,
                 fields, weight, itable, ftable, slot_of, tiles_of, south_of, north_of, tbuf, mats, t32, w0, w1, w2, w3, relay, o32, load_sem, halo_sem, send_sem, recv_sem):
    lon = lax.axis_index("lon")
    lat = lax.axis_index("lat")
    odd = (lon & 1) == 1
    far_z = (lon & 2) == 2
    polar = lat == 0
    relays = (lat == SIDES[0][1]) | (lat == SIDES[1][1])
    wins = (w0, w1, w2, w3)

    def at(lat_index, dist):
        return ((lon + dist) & (LON - 1), lat_index)

    def pick(if_odd, if_even):
        return jnp.where(odd, if_odd, if_even)

    north = (lat - 1) & (LAT - 1)
    south = (lat + 1) & (LAT - 1)
    sib = at(lat, pick(-1, 1))
    nb = at(lat, pick(1, -1))
    zdist = jnp.where(far_z, -2, 2)
    xdist = jnp.where(far_z, -4, 4)

    load_tracers = pltpu.make_async_copy(tracers, tbuf, load_sem.at[0])
    load_tracers.start()
    loads = [
        pltpu.make_async_copy(src, dst, load_sem.at[1 + i])
        for i, (src, dst) in enumerate(
            ((interp, mats), (lat_row_in, fields.at[0]), (lon_offset_in, fields.at[1]), (lat_weight_in, weight)))
    ]

    barrier = pltpu.get_barrier_semaphore()
    even = jnp.logical_not(odd)
    inner = odd != far_z
    outer = jnp.logical_not(inner)
    one = jnp.int32(1)
    none = jnp.int32(0)

    def greet(*devices):
        for d in devices:
            pl.semaphore_signal(barrier, inc=1, device_id=d, device_id_type=MESH)

    top = lat == 0
    bottom = lat == LAT - 1
    pl.when(jnp.logical_not(top))(lambda: greet((lon, north)))
    pl.when(jnp.logical_not(bottom))(lambda: greet((lon, south)))

    @pl.when(polar)
    def _():
        greet(sib, at(lat, zdist), at(lat, pick(2, -2)), at(lat, -xdist), at(lat, pick(4, -4)), at(1, pick(3, -3) + zdist),
              at(1, zdist + 8), at(lat, 8))
        pl.when(outer)(lambda: greet(nb))
        pl.when(odd)(lambda: greet(at(lat, 9)))
        for _, band, _ in SIDES:
            greet(at(band, 8), at(band, 0))
            pl.when(even)(lambda band=band: greet(at(band, jnp.where(far_z, 8, 4))))

    @pl.when(jnp.logical_not(polar))
    def _():
        greet(sib, nb)

    @pl.when(relays)
    def _():
        greet(at(0, 0), at(0, pick(1, -1)))
        pl.when(even)(lambda: greet(at(0, jnp.where(far_z, -1, 3))))

    @pl.when(lat == 1)
    def _():
        greet(at(0, zdist))

    load_tracers.wait()
    for load in loads:
        load.start()
    for g in range(BLOCKS):
        for rb in range(ROWS // 16):
            for ch in range(CH):
                part = tbuf[ch, 16 * rb : 16 * rb + 16, BLK * g : BLK * (g + 1)].astype(jnp.float32)
                t32[g, pl.ds(8 + 128 * rb + ch, 16, stride=8), :] = part

    def pack(q, low, high):
        own = jnp.where(polar, POLAR_OWN[q], 1)
        for g in range(BLOCKS):
            wins[q][own + g, low:high, :] = t32[g, 8 * QROWS * q + low : 8 * QROWS * q + high, :].astype(jnp.bfloat16)

    pack(1, 0, TILE_ROWS)
    pack(2, 0, TILE_ROWS)

    greeted = 4 - jnp.where(top | bottom, one, none) + jnp.where(polar, 9 + jnp.where(outer, one, none) + jnp.where(even, one, 2 * one), none)
    greeted = greeted + jnp.where(lat == 1, 2 * one, none) + jnp.where(relays, 2 + jnp.where(even, one, none), none)
    pl.semaphore_wait(barrier, greeted)

    down = pltpu.make_async_remote_copy(
        src_ref=t32.at[:, pl.ds(8 * ROWS, 8), :], dst_ref=t32.at[:, pl.ds(0, 8), :],
        send_sem=halo_sem.at[0], recv_sem=halo_sem.at[1], device_id=(lon, south), device_id_type=MESH)
    up = pltpu.make_async_remote_copy(
        src_ref=t32.at[:, pl.ds(8, 8), :], dst_ref=t32.at[:, pl.ds(8 * RIM - 8, 8), :],
        send_sem=halo_sem.at[2], recv_sem=halo_sem.at[3], device_id=(lon, north), device_id_type=MESH)
    pl.when(jnp.logical_not(bottom))(lambda: down.start())
    pl.when(jnp.logical_not(top))(lambda: up.start())

    ids = {}
    sent = []

    def copy(name, src, dst, to):
        index = ids.setdefault(name, len(ids))
        assert index < SEMS, name
        return pltpu.make_async_remote_copy(
            src_ref=src, dst_ref=dst, send_sem=send_sem.at[index], recv_sem=recv_sem.at[index],
            device_id=to, device_id_type=MESH)

    def when(cond, body):
        if cond is None:
            body()
        else:
            pl.when(cond)(body)

    def span(ref, first, count):
        return ref, first, count

    def block_of(slots):
        ref, first, count = slots
        return ref.at[pl.ds(first, count)]

    def put(name, src, dst, to, cond=None):
        when(cond, lambda: copy(name, block_of(src), block_of(dst), to).start())
        sent.append((name, src[0], src[2], cond))

    def got(name, dst, cond=None):
        when(cond, lambda: copy(name, block_of(dst), block_of(dst), sib).wait_recv())

    def all_sent_of(entry):
        name, ref, count, cond = entry
        block = ref.at[pl.ds(0, count)]
        when(cond, lambda: copy(name, block, block, sib).wait_send())

    def all_sent():
        for entry in sent:
            all_sent_of(entry)
        sent.clear()

    compute = functools.partial(interpolate, slot_of, tiles_of, south_of, north_of, mats, out, o32)
    pairs = range(0, BLOCKS, 2)

    def tabulate():
        for load in loads:
            load.wait()

        row = lax.broadcasted_iota(jnp.int32, (BLOCKS, ROWS), 1)
        shift = jnp.where(row < QROWS, POLAR_SHIFT[0], jnp.where(row < 2 * QROWS, POLAR_SHIFT[1], POLAR_SHIFT[2]))
        shift = jnp.where(polar, shift, 1)
        back = fields[0] < lat * ROWS + row
        odd_row = (row & 1) == 1
        itable[0] = jnp.maximum(shift + fields[1] + lax.broadcasted_iota(jnp.int32, (BLOCKS, ROWS), 0), 0)
        itable[1] = jnp.where(back, 0, 8) + jnp.where(odd_row, 8, 0)
        first_south = back != odd_row
        ftable[0] = jnp.where(first_south, 1.0 - weight[...], weight[...])
        ftable[1] = jnp.where(first_south, weight[...], 1.0 - weight[...])
        tables = [
            pltpu.make_async_copy(src, dst, load_sem.at[5 + i])
            for i, (src, dst) in enumerate(
                ((itable.at[0], slot_of), (itable.at[1], tiles_of), (ftable.at[0], south_of), (ftable.at[1], north_of)))
        ]
        for table in tables:
            table.start()
        for table in tables:
            table.wait()

    def across_c(q):
        for i in range(2):
            for side, _, firsts in SIDES:
                split = (q, i) == (3, 1)
                got(f"c{q} {side}{i} down", span(wins[q], pick(17, 1) + firsts[i], 2), inner if split else None)
                if split:
                    got(f"c3 nb{side}", span(w3, pick(17, 1) + firsts[i], 2), outer)
        put(f"c{q} one", span(wins[q], pick(17, 8), 1), span(wins[q], pick(25, 0), 1), sib)

    def finish_c(q):
        got(f"c{q} sib", span(wins[q], pick(1, 17), 8))
        got(f"c{q} end", span(wins[q], pick(25, 0), 1))
        got(f"c{q} one", span(wins[q], pick(0, 25), 1))

    def pass_x(i):
        far = jnp.where(far_z, 41, 9) + i
        got(f"b x{i}", span(w1, far, 2))
        put(f"b fx{i}", span(w1, far, 2), span(w1, jnp.where(far_z, pick(49, 33), pick(17, 1)) + i, 2), sib)

    @pl.when(polar)
    def _():
        def up_c(q, i):
            cond = inner if (q, i) == (3, 1) else None
            for side, band, firsts in SIDES:
                put(f"c{q} {side}{i} up", span(wins[q], 9 + firsts[i], 2), span(relay, 8 + 4 * (q - 2) + 2 * i, 2),
                    at(band, pick(1, -1)), cond)
                if cond is not None:
                    put(f"c3 nb{side}", span(w3, 9 + firsts[i], 2), span(w3, pick(1, 17) + firsts[i], 2), nb, outer)

        def up_a7(i):
            for side, band, firsts in SIDES:
                put(f"a7 {side}{i} up", span(w0, 17 + firsts[i], 2), span(relay, 4 + 2 * i, 2),
                    at(band, jnp.where(far_z, -3, 1)), odd)

        def up_a8(ways):
            for way, band, first, count, slot in PIECES:
                if way not in ways:
                    continue
                if way == "x":
                    put(f"a8 {first} down", span(w0, 17 + first, count), span(w0, 8 + first, count), at(band, -8))
                else:
                    put(f"a8 {first} up", span(w0, 17 + first, count), span(relay, slot, count), at(band, zdist if way == "z" else 0))

        def left(*names):
            for name in names:
                for entry in [x for x in sent if x[0] == name]:
                    sent.remove(entry)
                    all_sent_of(entry)

        for i in pairs:
            put(f"b z{i}", span(w1, 25 + i, 2), span(w1, jnp.where(far_z, 41, 9) + i, 2), at(lat, zdist))
        up_c(2, 0)
        up_c(2, 1)
        for i in pairs:
            put(f"b far{i} up", span(w1, pick(31 - i, 25 + i), 2), span(relay, i, 2), at(1, zdist))
        put("b end", span(w1, pick(25, 32), 1), span(w1, pick(57, 0), 1), at(lat, pick(-4, 4)))
        put("b sib", span(w1, 25, 8), span(w1, pick(33, 17), 8), sib)
        put("c2 sib", span(w2, 9, 8), span(w2, pick(17, 1), 8), sib)
        put("c2 end", span(w2, pick(9, 16), 1), span(w2, pick(25, 0), 1), at(lat, pick(-2, 2)))

        for g in range(BLOCKS):
            first = t32[g, 8:16, :]
            w0[17 + g, 0:16, :] = jnp.concatenate([jnp.zeros_like(first), first], axis=0).astype(jnp.bfloat16)
        pack(0, 16, TILE_ROWS)
        up_a8(("x", "z"))
        put("a9", span(w0, 17, 1), span(w0, 16, 1), at(lat, -9), even)

        pack(3, 0, TILE_ROWS - 16)
        down.wait_send()
        up.wait_recv()
        pack(3, TILE_ROWS - 16, TILE_ROWS)
        put("c3 sib", span(w3, 9, 8), span(w3, pick(17, 1), 8), sib)
        put("c3 end", span(w3, pick(9, 16), 1), span(w3, pick(25, 0), 1), at(lat, pick(-2, 2)))

        for i in pairs:
            mine = span(w1, jnp.where(far_z, 9, 41) + i, 2)
            got(f"b z{i}", mine)
            put(f"b x{i}", mine, span(w1, jnp.where(far_z, 41, 9) + i, 2), at(lat, xdist))
            put(f"b fz{i}", mine, span(w1, jnp.where(far_z, pick(17, 1), pick(49, 33)) + i, 2), sib)
            if i == 0:
                left("c2 n0 up", "c2 s0 up")
                up_a8(("n", "s"))
                up_a7(0)
                tabulate()
            if i == 2:
                left("c2 n1 up", "c2 s1 up")
                up_a7(1)
                up_c(3, 0)
            if i == 4:
                left("a7 n1 up", "a7 s1 up")
                up_c(3, 1)
            if i >= 4:
                pass_x(i - 4)
            if i == 4:
                across_c(2)
        finish_c(2)

    polar_sent = list(sent)
    sent.clear()

    @pl.when(jnp.logical_not(polar))
    def _():
        def sides(q):
            put(f"left {q}", span(wins[q], 1, 1), span(wins[q], 9, 1), at(lat, -1))
            put(f"right {q}", span(wins[q], 8, 1), span(wins[q], 0, 1), at(lat, 1))

        passed = []

        def on_the_way(stage):
            plain = list(sent)

            def pass_on(name, slot, count, win, first, dist, cond=None):
                block = span(relay, slot, count)
                got(f"{name} up", block, cond)
                put(f"{name} down", block, span(win, first, count), at(0, dist), cond)

            @pl.when(lat == 1)
            def _():
                sent.clear()
                if stage == 0:
                    pass_on("b far0", 0, 2, w1, pick(7, 49), zdist + pick(3, -3))
                else:
                    for i in pairs[1:]:
                        pass_on(f"b far{i}", i, 2, w1, pick(7 - i, 49 + i), zdist + pick(3, -3))
                    for way, _, first, count, slot in PIECES:
                        if way == "z":
                            pass_on(f"a8 {first}", slot, count, w0, 8 + first, zdist - 8)
                passed.extend((1, x) for x in sent)

            for side, band, firsts in SIDES:
                @pl.when(lat == band)
                def _(side=side, band=band, firsts=firsts):
                    sent.clear()
                    if stage == 0:
                        for i in range(2):
                            pass_on(f"c2 {side}{i}", 8 + 2 * i, 2, w2, pick(17, 1) + firsts[i], 0)
                    else:
                        for way, _, first, count, slot in PIECES:
                            if way == side:
                                pass_on(f"a8 {first}", slot, count, w0, 8 + first, -8)
                        for i in range(2):
                            pass_on(f"a7 {side}{i}", 4 + 2 * i, 2, w0, firsts[i], jnp.where(far_z, -8, -4), even)
                        for i in range(2):
                            pass_on(f"c3 {side}{i}", 12 + 2 * i, 2, w3, pick(17, 1) + firsts[i], 0, inner if i else None)
                    passed.extend((band, x) for x in sent)

            sent.clear()
            sent.extend(plain)

        sides(1)
        sides(2)
        on_the_way(0)
        pack(0, 16, TILE_ROWS)
        pack(3, 0, TILE_ROWS - 16)
        up.wait_send()
        down.wait_recv()

        @pl.when(jnp.logical_not(bottom))
        def _():
            down.wait_send()
            up.wait_recv()

        @pl.when(bottom)
        def _():
            t32[:, 8 * RIM - 8 : 8 * RIM, :] = jnp.zeros((BLOCKS, 8, BLK), jnp.float32)

        pack(0, 0, 16)
        pack(3, TILE_ROWS - 16, TILE_ROWS)
        sides(0)
        sides(3)
        tabulate()
        on_the_way(1)
        plain = list(sent)
        for band in (1, 2, 6):
            @pl.when(lat == band)
            def _(band=band):
                sent.clear()
                sent.extend(x for at_band, x in passed if at_band == band)
                all_sent()

        sent.clear()
        sent.extend(plain)

        for q in range(4):
            got(f"left {q}", span(wins[q], 9, 1))
            got(f"right {q}", span(wins[q], 0, 1))

    plain_sent = list(sent)
    sent.clear()
    sent.extend(polar_sent)

    compute(2, w2)

    @pl.when(polar)
    def _():
        pass_x(4)
        got("b far0 down", span(w1, pick(49, 7), 2))
        put("b one", span(w1, pick(49, 8), 1), span(w1, pick(57, 0), 1), sib)
        for _, _, first, count, _ in PIECES:
            got(f"a8 {first} down", span(w0, 8 + first, count))
            put(f"a f {first}", span(w0, 8 + first, count), span(w0, first, count), sib, even)
            if first == 0:
                put("a one", span(w0, 8, 1), span(w0, 16, 1), sib, odd)
        pass_x(6)
        for i in pairs[1:]:
            got(f"b far{i} down", span(w1, pick(49 + i, 7 - i), 2))
        got("b end", span(w1, pick(57, 0), 1))
        got("b sib", span(w1, pick(17, 33), 8))
        for i in pairs:
            got(f"b fz{i}", span(w1, jnp.where(far_z, pick(1, 17), pick(33, 49)) + i, 2))
            got(f"b fx{i}", span(w1, jnp.where(far_z, pick(33, 49), pick(1, 17)) + i, 2))
        got("b one", span(w1, pick(0, 57), 1))

    compute(1, w1)

    @pl.when(polar)
    def _():
        across_c(3)
        for i in range(2):
            for side, _, firsts in SIDES:
                got(f"a7 {side}{i} down", span(w0, firsts[i], 2), even)
        for _, _, first, count, _ in PIECES:
            got(f"a f {first}", span(w0, first, count), odd)
        got("a9", span(w0, 16, 1), odd)
        got("a one", span(w0, 16, 1), even)

    compute(0, w0)

    @pl.when(polar)
    def _():
        finish_c(3)

    compute(3, w3)

    @pl.when(polar)
    def _():
        all_sent()

    sent.extend(plain_sent)

    @pl.when(jnp.logical_not(polar))
    def _():
        all_sent()


def interpolate(slot_of, tiles_of, south_of, north_of, mats, out, o32, q, window):
    sublane = lax.broadcasted_iota(jnp.int32, (16, BLK), 0)

    def part_of_rows(part, carry):
        for j in range(16):
            start = pl.multiple_of(128 * part + 16 * (j // 2), 16)
            row = QROWS * q + 16 * part + j
            lead, trail = [], []
            for b in range(BLOCKS):
                g = slot_of[b, row]
                lower = sublane < tiles_of[b, row]
                for tiles, slot in ((lead, g), (trail, g + 1)):
                    tiles.append(jnp.where(lower, window[slot, pl.ds(start + 16, 16), :], window[slot, pl.ds(start, 16), :]))
            lhs = jnp.concatenate([jnp.concatenate(lead, axis=0), jnp.concatenate(trail, axis=0)], axis=1)
            prod = jnp.dot(lhs, mats[row], preferred_element_type=jnp.float32)
            for b in range(BLOCKS):
                at = 16 * b
                o32[b, 8 * j : 8 * j + 8, :] = south_of[b, row] * prod[at : at + 8] + north_of[b, row] * prod[at + 8 : at + 16]
        low = pl.multiple_of(QROWS * q + 16 * part, 16)
        for b in range(BLOCKS):
            for ch in range(CH):
                out[ch, pl.ds(low, 16), BLK * b : BLK * (b + 1)] = o32[b, pl.ds(ch, 16, stride=8), :].astype(jnp.bfloat16)
        return carry

    lax.fori_loop(0, 2, part_of_rows, 0)


def on_device(tracers, interp, lat_weight, lat_row, lon_offset):
    packed = tracers.reshape(CH, ROWS, BLOCKS * BLK)
    anywhere = pl.BlockSpec(memory_space=pl.ANY)
    result = pl.pallas_call(
        fused_kernel,
        out_shape=pltpu.VMEM((CH, ROWS, BLOCKS * BLK), jnp.bfloat16),
        in_specs=[anywhere] * 5,
        out_specs=pl.BlockSpec(memory_space=pltpu.VMEM),
        scratch_shapes=[
            pltpu.VMEM((2, BLOCKS, ROWS), jnp.int32),
            pltpu.VMEM((BLOCKS, ROWS), jnp.float32),
            pltpu.VMEM((2, BLOCKS, ROWS), jnp.int32),
            pltpu.VMEM((2, BLOCKS, ROWS), jnp.float32),
            pltpu.SMEM((BLOCKS, ROWS), jnp.int32),
            pltpu.SMEM((BLOCKS, ROWS), jnp.int32),
            pltpu.SMEM((BLOCKS, ROWS), jnp.float32),
            pltpu.SMEM((BLOCKS, ROWS), jnp.float32),
            pltpu.VMEM((CH, ROWS, BLOCKS * BLK), jnp.bfloat16),
            pltpu.VMEM((ROWS, 2 * BLK, BLK), jnp.bfloat16),
            pltpu.VMEM((BLOCKS, 8 * RIM, BLK), jnp.float32),
        ] + [pltpu.VMEM((n, TILE_ROWS, BLK), jnp.bfloat16) for n in SLOTS] + [
            pltpu.VMEM((RELAY, TILE_ROWS, BLK), jnp.bfloat16),
            pltpu.VMEM((BLOCKS, 8 * 16, BLK), jnp.float32),
            pltpu.SemaphoreType.DMA((9,)),
            pltpu.SemaphoreType.DMA((4,)),
            pltpu.SemaphoreType.DMA((SEMS,)),
            pltpu.SemaphoreType.DMA((SEMS,)),
        ],
        compiler_params=pltpu.CompilerParams(collective_id=0, has_side_effects=True, vmem_limit_bytes=56 << 20),
        name="advect",
    )(lat_row.T, lon_offset.T, lat_weight.T, packed, interp)
    return result.reshape(tracers.shape)


def solution(mesh):
    return jax.shard_map(
        on_device,
        mesh=mesh,
        in_specs=(
            P(None, None, "lat", "lon"),
            P("lat", None, None),
            P("lat", "lon"),
            P("lat", "lon"),
            P("lat", "lon"),
        ),
        out_specs=P(None, None, "lat", "lon"),
        check_vma=False,
    )
```

time: 51.9 us -> 42.7 us (0.82)
  Pallas kernels: 50 us -> 41.2 us
    pallas_call x1, Pallas kernels: 47 us -> 41.2 us  [on_device(): pl.pallas_call(fused_kernel, out_shape=pltpu.VMEM((CH, ROWS, BLOCKS * BLK...]
    pallas_call x1 -> x0, Pallas kernels: 2.92 us -> none  [on_device(): pl.pallas_call(store_kernel, out_shape=jax.ShapeDtypeStruct((CH, ROWS, BL...]
    unnamed x2 -> x1, local copies, waits for them, and re-layouts: 1.34 us -> 1.32 us
where the time goes in v5:
time: 42.7 us; the launch traced here: 42.5 us
  Pallas kernels  41.2 us (96%)
  local copies, waits for them, and re-layouts  1.32 us (3%)
    pallas_call x1, Pallas kernels, on_device(): pl.pallas_call(fused_kernel, out_shape=pltpu.VMEM((CH, ROWS, BLOCKS * BLK...  41.2 us
    unnamed x1, local copies, waits for them, and re-layouts  1.32 us

profile of v5, /device:TPU:1, one launch (start us, length us, event | category | flops | bytes accessed | tf_op | source)
XLA Modules:
  0.0 42.5 jit_solution(621376232160512326)
XLA Ops:
  0.0 41.2 %advect.1 = bf16[8,128,1024]{2,1,0:T(8,128)(2,1)S(1)} custom-call(s32[8,128]{1,0:T(8,128)} %bitcast.7, s32[8,128]{1,0:T(8,128)} %bitcast.8, f32[8,128]{1,0:T(8,128)} %bitcast.9, bf16[8,128,1024]{2,1,0:T(8,128)(2,1)} %bitcast.6, bf16[128,256,128]{2,1,0:T(8,128)(2,1)} %interp.1), custom_call_target="tpu_custom_call" | custom-call | tf_op jit(solution)/shard_map/advect/pallas_call | solution.py:472
  41.2 1.3 %copy.7 = bf16[2,4,128,1024]{3,2,1,0:T(8,128)(2,1)} copy(bf16[2,4,128,1024]{3,2,1,0:T(8,128)(2,1)S(1)} %bitcast.5) | data formatting | bytes 4194304

commit v6 on v5

--- a/solution.py
+++ b/solution.py
@@ -21,8 +21,9 @@
 POLAR_OWN = (17, 25, 9, 9)
 SLOTS = (25, 58, 26, 26)
 SIDES = (("n", 2, (0, 2)), ("s", 6, (4, 6)))
-PIECES = (("x", 0, 0, 4, 0), ("n", 2, 4, 1, 0), ("s", 6, 5, 1, 0), ("z", 1, 6, 2, 8))
-SEMS = 128
+PIECES = (("x", 0, 0, 6, 0), ("z", 1, 6, 2, 8))
+SENDS = 51
+LANDS = 51
 RELAY = 16
 MESH = pl.DeviceIdType.MESH
 
@@ -127,15 +128,26 @@
     pl.when(jnp.logical_not(bottom))(lambda: down.start())
     pl.when(jnp.logical_not(top))(lambda: up.start())
 
-    ids = {}
+    started = ({}, {})
+    landed = ({}, {})
     sent = []
 
+    def number(names, name, most):
+        index = names.setdefault(name, len(names))
+        assert index < most, name
+        return index
+
     def copy(name, src, dst, to):
-        index = ids.setdefault(name, len(ids))
-        assert index < SEMS, name
+        plain = name.startswith(("left", "right"))
+        from_polar = not plain and (not name.endswith("down") or name in direct)
+        to_polar = not plain and not name.endswith("up")
         return pltpu.make_async_remote_copy(
-            src_ref=src, dst_ref=dst, send_sem=send_sem.at[index], recv_sem=recv_sem.at[index],
+            src_ref=src, dst_ref=dst,
+            send_sem=send_sem.at[number(started[from_polar], name, SENDS)],
+            recv_sem=recv_sem.at[number(landed[to_polar], name, LANDS)],
             device_id=to, device_id_type=MESH)
+
+    direct = [f"a8 {first} down" for way, _, first, _, _ in PIECES if way == "x"]
 
     def when(cond, body):
         if cond is None:
@@ -197,10 +209,10 @@
     def across_c(q):
         for i in range(2):
             for side, _, firsts in SIDES:
-                split = (q, i) == (3, 1)
+                split = q == 3
                 got(f"c{q} {side}{i} down", span(wins[q], pick(17, 1) + firsts[i], 2), inner if split else None)
                 if split:
-                    got(f"c3 nb{side}", span(w3, pick(17, 1) + firsts[i], 2), outer)
+                    got(f"c3 nb{firsts[i]}", span(w3, pick(17, 1) + firsts[i], 2), outer)
         put(f"c{q} one", span(wins[q], pick(17, 8), 1), span(wins[q], pick(25, 0), 1), sib)
 
     def finish_c(q):
@@ -216,12 +228,10 @@
     @pl.when(polar)
     def _():
         def up_c(q, i):
-            cond = inner if (q, i) == (3, 1) else None
+            cond = inner if q == 3 else None
             for side, band, firsts in SIDES:
                 put(f"c{q} {side}{i} up", span(wins[q], 9 + firsts[i], 2), span(relay, 8 + 4 * (q - 2) + 2 * i, 2),
                     at(band, pick(1, -1)), cond)
-                if cond is not None:
-                    put(f"c3 nb{side}", span(w3, 9 + firsts[i], 2), span(w3, pick(1, 17) + firsts[i], 2), nb, outer)
 
         def up_a7(i):
             for side, band, firsts in SIDES:
@@ -280,11 +290,12 @@
                 tabulate()
             if i == 2:
                 left("c2 n1 up", "c2 s1 up")
-                up_a7(1)
                 up_c(3, 0)
             if i == 4:
-                left("a7 n1 up", "a7 s1 up")
+                up_a7(1)
                 up_c(3, 1)
+                for k in pairs:
+                    put(f"c3 nb{k}", span(w3, 9 + k, 2), span(w3, pick(1, 17) + k, 2), nb, outer)
             if i >= 4:
                 pass_x(i - 4)
             if i == 4:
@@ -336,8 +347,7 @@
                                 pass_on(f"a8 {first}", slot, count, w0, 8 + first, -8)
                         for i in range(2):
                             pass_on(f"a7 {side}{i}", 4 + 2 * i, 2, w0, firsts[i], jnp.where(far_z, -8, -4), even)
-                        for i in range(2):
-                            pass_on(f"c3 {side}{i}", 12 + 2 * i, 2, w3, pick(17, 1) + firsts[i], 0, inner if i else None)
+                            pass_on(f"c3 {side}{i}", 12 + 2 * i, 2, w3, pick(17, 1) + firsts[i], 0, inner)
                     passed.extend((band, x) for x in sent)
 
             sent.clear()
@@ -389,6 +399,7 @@
 
     @pl.when(polar)
     def _():
+        early = list(sent)
         pass_x(4)
         got("b far0 down", span(w1, pick(49, 7), 2))
         put("b one", span(w1, pick(49, 8), 1), span(w1, pick(57, 0), 1), sib)
@@ -397,7 +408,30 @@
             put(f"a f {first}", span(w0, 8 + first, count), span(w0, first, count), sib, even)
             if first == 0:
                 put("a one", span(w0, 8, 1), span(w0, 16, 1), sib, odd)
+        for entry in early:
+            if not entry[0].startswith(("c3 nb", "b x6", "b fz6", "c3 n1", "c3 s1")):
+                sent.remove(entry)
+                all_sent_of(entry)
         pass_x(6)
+        across_c(3)
+        for i in range(2):
+            for side, _, firsts in SIDES:
+                got(f"a7 {side}{i} down", span(w0, firsts[i], 2), even)
+        for _, _, first, count, _ in PIECES:
+            got(f"a f {first}", span(w0, first, count), odd)
+        got("a9", span(w0, 16, 1), odd)
+        got("a one", span(w0, 16, 1), even)
+
+    compute(0, w0)
+
+    @pl.when(polar)
+    def _():
+        finish_c(3)
+
+    compute(3, w3)
+
+    @pl.when(polar)
+    def _():
         for i in pairs[1:]:
             got(f"b far{i} down", span(w1, pick(49 + i, 7 - i), 2))
         got("b end", span(w1, pick(57, 0), 1))
@@ -411,25 +445,6 @@
 
     @pl.when(polar)
     def _():
-        across_c(3)
-        for i in range(2):
-            for side, _, firsts in SIDES:
-                got(f"a7 {side}{i} down", span(w0, firsts[i], 2), even)
-        for _, _, first, count, _ in PIECES:
-            got(f"a f {first}", span(w0, first, count), odd)
-        got("a9", span(w0, 16, 1), odd)
-        got("a one", span(w0, 16, 1), even)
-
-    compute(0, w0)
-
-    @pl.when(polar)
-    def _():
-        finish_c(3)
-
-    compute(3, w3)
-
-    @pl.when(polar)
-    def _():
         all_sent()
 
     sent.extend(plain_sent)
@@ -442,9 +457,9 @@
 def interpolate(slot_of, tiles_of, south_of, north_of, mats, out, o32, q, window):
     sublane = lax.broadcasted_iota(jnp.int32, (16, BLK), 0)
 
-    def part_of_rows(part, carry):
+    for part in range(2):
         for j in range(16):
-            start = pl.multiple_of(128 * part + 16 * (j // 2), 16)
+            start = 128 * part + 16 * (j // 2)
             row = QROWS * q + 16 * part + j
             lead, trail = [], []
             for b in range(BLOCKS):
@@ -457,13 +472,10 @@
             for b in range(BLOCKS):
                 at = 16 * b
                 o32[b, 8 * j : 8 * j + 8, :] = south_of[b, row] * prod[at : at + 8] + north_of[b, row] * prod[at + 8 : at + 16]
-        low = pl.multiple_of(QROWS * q + 16 * part, 16)
+        low = QROWS * q + 16 * part
         for b in range(BLOCKS):
             for ch in range(CH):
-                out[ch, pl.ds(low, 16), BLK * b : BLK * (b + 1)] = o32[b, pl.ds(ch, 16, stride=8), :].astype(jnp.bfloat16)
-        return carry
-
-    lax.fori_loop(0, 2, part_of_rows, 0)
+                out[ch, low : low + 16, BLK * b : BLK * (b + 1)] = o32[b, pl.ds(ch, 16, stride=8), :].astype(jnp.bfloat16)
 
 
 def on_device(tracers, interp, lat_weight, lat_row, lon_offset):
@@ -491,8 +503,8 @@
             pltpu.VMEM((BLOCKS, 8 * 16, BLK), jnp.float32),
             pltpu.SemaphoreType.DMA((9,)),
             pltpu.SemaphoreType.DMA((4,)),
-            pltpu.SemaphoreType.DMA((SEMS,)),
-            pltpu.SemaphoreType.DMA((SEMS,)),
+            pltpu.SemaphoreType.DMA((SENDS,)),
+            pltpu.SemaphoreType.DMA((LANDS,)),
         ],
         compiler_params=pltpu.CompilerParams(collective_id=0, has_side_effects=True, vmem_limit_bytes=56 << 20),
         name="advect",

time: 42.7 us -> 39 us (0.913)
  Pallas kernels: 41.2 us -> 37.6 us
    pallas_call x1, Pallas kernels: 41.2 us -> 37.6 us  [on_device(): pl.pallas_call(fused_kernel, out_shape=pltpu.VMEM((CH, ROWS, BLOCKS * BLK...]
where the time goes in v6:
time: 39 us; the launch traced here: 38.9 us
  Pallas kernels  37.6 us (96%)
  local copies, waits for them, and re-layouts  1.32 us (3%)
    pallas_call x1, Pallas kernels, on_device(): pl.pallas_call(fused_kernel, out_shape=pltpu.VMEM((CH, ROWS, BLOCKS * BLK...  37.6 us
    unnamed x1, local copies, waits for them, and re-layouts  1.32 us

profile of v6, /device:TPU:1, one launch (start us, length us, event | category | flops | bytes accessed | tf_op | source)
XLA Modules:
  0.0 38.9 jit_solution(9905845086239907209)
XLA Ops:
  0.0 37.6 %advect.1 = bf16[8,128,1024]{2,1,0:T(8,128)(2,1)S(1)} custom-call(s32[8,128]{1,0:T(8,128)} %bitcast.7, s32[8,128]{1,0:T(8,128)} %bitcast.8, f32[8,128]{1,0:T(8,128)} %bitcast.9, bf16[8,128,1024]{2,1,0:T(8,128)(2,1)} %bitcast.6, bf16[128,256,128]{2,1,0:T(8,128)(2,1)} %interp.1), custom_call_target="tpu_custom_call" | custom-call | tf_op jit(solution)/shard_map/advect/pallas_call | solution.py:484
  37.6 1.3 %copy.7 = bf16[2,4,128,1024]{3,2,1,0:T(8,128)(2,1)} copy(bf16[2,4,128,1024]{3,2,1,0:T(8,128)(2,1)S(1)} %bitcast.5) | data formatting | bytes 4194304

commit v7 on v6

--- a/solution.py
+++ b/solution.py
@@ -257,8 +257,11 @@
             put(f"b z{i}", span(w1, 25 + i, 2), span(w1, jnp.where(far_z, 41, 9) + i, 2), at(lat, zdist))
         up_c(2, 0)
         up_c(2, 1)
-        for i in pairs:
-            put(f"b far{i} up", span(w1, pick(31 - i, 25 + i), 2), span(relay, i, 2), at(1, zdist))
+        def up_far(*firsts):
+            for i in firsts:
+                put(f"b far{i} up", span(w1, pick(31 - i, 25 + i), 2), span(relay, i, 2), at(1, zdist))
+
+        up_far(0, 2)
         put("b end", span(w1, pick(25, 32), 1), span(w1, pick(57, 0), 1), at(lat, pick(-4, 4)))
         put("b sib", span(w1, 25, 8), span(w1, pick(33, 17), 8), sib)
         put("c2 sib", span(w2, 9, 8), span(w2, pick(17, 1), 8), sib)
@@ -269,6 +272,7 @@
             w0[17 + g, 0:16, :] = jnp.concatenate([jnp.zeros_like(first), first], axis=0).astype(jnp.bfloat16)
         pack(0, 16, TILE_ROWS)
         up_a8(("x", "z"))
+        up_far(4, 6)
         put("a9", span(w0, 17, 1), span(w0, 16, 1), at(lat, -9), even)
 
         pack(3, 0, TILE_ROWS - 16)
@@ -329,9 +333,9 @@
                 else:
                     for i in pairs[1:]:
                         pass_on(f"b far{i}", i, 2, w1, pick(7 - i, 49 + i), zdist + pick(3, -3))
-                    for way, _, first, count, slot in PIECES:
-                        if way == "z":
-                            pass_on(f"a8 {first}", slot, count, w0, 8 + first, zdist - 8)
+                        for way, _, first, count, slot in PIECES:
+                            if way == "z" and i == 2:
+                                pass_on(f"a8 {first}", slot, count, w0, 8 + first, zdist - 8)
                 passed.extend((1, x) for x in sent)
 
             for side, band, firsts in SIDES:

time: 39 us -> 38.9 us (level)
  no operation moved by 1% of the time
where the time goes in v7:
time: 38.9 us; the launch traced here: 38.7 us
  Pallas kernels  37.4 us (96%)
  local copies, waits for them, and re-layouts  1.32 us (3%)
    pallas_call x1, Pallas kernels, on_device(): pl.pallas_call(fused_kernel, out_shape=pltpu.VMEM((CH, ROWS, BLOCKS * BLK...  37.4 us
    unnamed x1, local copies, waits for them, and re-layouts  1.32 us

profile of v7, /device:TPU:1, one launch (start us, length us, event | category | flops | bytes accessed | tf_op | source)
XLA Modules:
  0.0 38.7 jit_solution(2545217071522118013)
XLA Ops:
  0.0 37.4 %advect.1 = bf16[8,128,1024]{2,1,0:T(8,128)(2,1)S(1)} custom-call(s32[8,128]{1,0:T(8,128)} %bitcast.7, s32[8,128]{1,0:T(8,128)} %bitcast.8, f32[8,128]{1,0:T(8,128)} %bitcast.9, bf16[8,128,1024]{2,1,0:T(8,128)(2,1)} %bitcast.6, bf16[128,256,128]{2,1,0:T(8,128)(2,1)} %interp.1), custom_call_target="tpu_custom_call" | custom-call | tf_op jit(solution)/shard_map/advect/pallas_call | solution.py:488
  37.4 1.3 %copy.7 = bf16[2,4,128,1024]{3,2,1,0:T(8,128)(2,1)} copy(bf16[2,4,128,1024]{3,2,1,0:T(8,128)(2,1)S(1)} %bitcast.5) | data formatting | bytes 4194304
